TPU v7x, 512 devices: a whole 4x8x8 slice. The times are simulated.
512 devices in a mesh: seq: 128 (over z, y, core), pack: 4 (over x).
Axes of the slice: x: 4, y: 8, z: 8, core: 2. Of those that a mesh axis runs over, the one named last changes fastest.
Arguments:
- queries: bfloat16 [131072, 2048], P(('pack', 'seq')), parts along dimension 0, may hold values from -10 to 10
- keys: bfloat16 [131072, 512], P(('pack', 'seq')), parts along dimension 0, may hold values from -10 to 10
- values: bfloat16 [131072, 512], P(('pack', 'seq')), parts along dimension 0, may hold values from -6 to 6
- lengths: int32 [512], P('pack'), parts along dimension 0, may hold values from 1 to 4096, 32768 in all
- home: int32 [1024], P('pack'), parts along dimension 0, may hold values from 0 to 127, as said below
Outputs:
- attended: bfloat16 [131072, 2048], P(('pack', 'seq')), parts along dimension 0
There are 4 independent parts, one for each index of `pack`. A program takes and returns all parts, laid end to end along the dimension named above; each array names one. Nothing has to cross between parts.
Inputs may be any that keep to these rules, and one draw needn't show every extreme that they name: Block b covers positions b * 128 to b * 128 + 127. home[b] is 2 * (b // 4) or that plus one, and every device index is home of exactly 2 blocks.
All inputs are finite; a program needn't handle non-finite values.
Results may differ from a plain program's by a relative error of at most 0.0033.
Values may be sent and summed in bfloat16 or wider, within the bound.
No kernel may reach another device: no remote copies, remote signals or barrier semaphores. Data moves between devices by JAX's collectives and lax.ppermute only.
A program may use at most 64 MiB of HBM per device.

v0:
```python
import jax
import jax.numpy as jnp
from jax import lax
from jax.sharding import PartitionSpec as P

HD = 128
BLOCK = 128
WIN_SHARDS = 8
TOK_DEV = 256


def shifted(value, axis, steps):
    count = lax.axis_size(axis)
    initial, last = (max(0, -steps), min(count, count - steps))
    return lax.ppermute(value, axis, [(source, source + steps) for source in range(initial, last)])


def partner_2(block, axis, distance):
    count = lax.axis_size(axis)
    route = []
    for low in range(count):
        high = low | 1 << distance
        if high != low and high < count:
            route += [(low, high), (high, low)]
    return lax.ppermute(block, axis, route)


def doc_first_of(lengths, positions):
    doc_ends = jnp.cumsum(lengths)
    doc_starts = doc_ends - lengths
    chosen = jnp.where(doc_starts[None, :] <= positions[:, None], doc_starts[None, :], 0)
    return jnp.max(chosen, axis=1)


def fold_piece(softmax_state, grouped, query_pos, doc_first, key_piece, key_start):
    key_count = key_piece.shape[1]
    kv_heads = grouped.shape[1]
    key_pos = key_start + jnp.arange(key_count, dtype=jnp.int32)
    allowed = (
        (key_pos[None, :] <= query_pos[:, None])
        & (key_pos[None, :] > query_pos[:, None] - WIN_SHARDS * TOK_DEV)
        & (key_pos[None, :] >= doc_first[:, None])
        & True
    )

    def update(previous):
        running_max, denominator, numerator = previous
        key_rows = key_piece[0].reshape(key_count, kv_heads, HD)
        value_rows = key_piece[1].reshape(key_count, kv_heads, HD)
        scores = jnp.einsum(
            "qhgd,khd->hgqk", grouped, key_rows, preferred_element_type=jnp.float32
        ) * HD ** (-0.5)
        scores = jnp.where(allowed, scores, jnp.float32(-1e30))
        new_max = jnp.maximum(running_max, jnp.max(scores, axis=-1))
        weights = jnp.where(allowed, jnp.exp(scores - new_max[..., None]), jnp.float32(0.0))
        rescale = jnp.exp(running_max - new_max)
        new_denominator = denominator * rescale + jnp.sum(weights, axis=-1)
        product = jnp.einsum(
            "hgqk,khd->hgqd",
            weights.astype(jnp.bfloat16),
            value_rows,
            preferred_element_type=jnp.float32,
        )
        new_numerator = numerator * rescale[..., None] + product
        return (new_max, new_denominator, new_numerator)

    return lax.cond(jnp.any(allowed), update, lambda previous: previous, softmax_state)


def context_fold(softmax_state, grouped, query_pos, doc_first, key_values, device_index, depth):
    row_count = key_values.shape[1]

    def advance(loop_carry, distance):
        key_piece, inner_state = loop_carry
        key_piece = shifted(key_piece, "seq", 1)
        inner_state = fold_piece(
            inner_state,
            grouped,
            query_pos,
            doc_first,
            key_piece,
            (device_index - distance) * row_count,
        )
        return ((key_piece, inner_state), None)

    (final_piece, softmax_state), unused = lax.scan(
        advance, (key_values, softmax_state), jnp.arange(1, depth + 1, dtype=jnp.int32)
    )
    return softmax_state


def empty_state(kv_heads, group_size, row_count):
    running_max = jnp.full((kv_heads, group_size, row_count), -1e30, jnp.float32)
    denominator = jnp.zeros((kv_heads, group_size, row_count), jnp.float32)
    numerator = jnp.zeros((kv_heads, group_size, row_count, HD), jnp.float32)
    return (running_max, denominator, numerator)


def finish(softmax_state, row_count):
    running_max, denominator, numerator = softmax_state
    mixed = numerator / denominator[..., None]
    return mixed.transpose(2, 0, 1, 3).reshape(row_count, -1).astype(jnp.bfloat16)


def selection(home, device_index, blocks_dev):
    group_base = device_index // 2 * 2 * blocks_dev
    group_home = lax.dynamic_slice_in_dim(home, group_base, 2 * blocks_dev, 0)
    owned = (group_home == device_index).astype(jnp.int32)
    ranks = jnp.cumsum(owned) - 1
    chooser = (
        (ranks[None, :] == jnp.arange(blocks_dev, dtype=jnp.int32)[:, None]) & (owned[None, :] == 1)
    ).astype(jnp.int32)
    chosen = group_base + jnp.sum(
        chooser * jnp.arange(2 * blocks_dev, dtype=jnp.int32)[None, :], axis=1
    )
    return (chooser, chosen)


def pick_blocks(chooser, lower_half, upper_half, blocks_dev):
    columns = lower_half.shape[1]
    group_rows = jnp.concatenate([lower_half, upper_half], axis=0).reshape(
        2 * blocks_dev, BLOCK * columns
    )
    picked = jnp.einsum(
        "jl,lx->jx", chooser.astype(jnp.bfloat16), group_rows, preferred_element_type=jnp.float32
    )
    return picked.astype(jnp.bfloat16).reshape(blocks_dev * BLOCK, columns)


def local(queries, keys, values, lengths, home):
    row_count = queries.shape[0]
    query_cols = queries.shape[1]
    kv_heads = keys.shape[1] // HD
    group_size = query_cols // HD // kv_heads
    blocks_dev = row_count // BLOCK
    device_index = lax.axis_index("seq")
    is_even = device_index % 2 == 0
    key_values = jnp.stack([keys, values])
    chooser, chosen = selection(home, device_index, blocks_dev)
    query_pos = device_index * row_count + jnp.arange(row_count, dtype=jnp.int32)
    doc_first = doc_first_of(lengths, query_pos)
    grouped = queries.reshape(row_count, kv_heads, group_size, HD)
    softmax_state = empty_state(kv_heads, group_size, row_count)
    softmax_state = fold_piece(
        softmax_state, grouped, query_pos, doc_first, key_values, device_index * row_count
    )
    softmax_state = context_fold(
        softmax_state, grouped, query_pos, doc_first, key_values, device_index, WIN_SHARDS
    )
    mixed = finish(softmax_state, row_count)
    partner = partner_2(mixed, "seq", 0)
    lower_half = jnp.where(is_even, mixed, partner)
    upper_half = jnp.where(is_even, partner, mixed)
    return pick_blocks(chooser, lower_half, upper_half, blocks_dev)


def solution(mesh):
    placed = (
        P(("pack", "seq"), None),
        P(("pack", "seq"), None),
        P(("pack", "seq"), None),
        P("pack"),
        P("pack"),
    )
    return jax.shard_map(
        local, mesh=mesh, in_specs=placed, out_specs=P(("pack", "seq"), None), check_vma=False
    )
```

profile of v0, /device:TPU:263, one launch (start us, length us, event | category | flops | bytes accessed | tf_op | source)
XLA Modules:
  0.0 209.2 jit_solution(9566982637520667649)
XLA Ops:
  0.0 0.8 copy.46
  1.8 1.5 copy.47
  4.4 0.8 compare_and_fusion.1
  5.9 0.8 pad_maximum_fusion.1
  6.7 10.7 %conditional.2 = (f32[4,4,256]{2,1,0:T(4,128)}, f32[4,4,256]{2,1,0:T(4,128)S(1)}, f32[4,4,256,128]{3,2,1,0:T(8,128)}) conditional(s32[]{:T(128)} %convert_element_type.39, () %tuple.32, (pred[256,256]{0,1:T(8,128)(4,1)S(1)}, bf16[256,512]{1,0:T(8,128)(2,1)S(1)}, bf16[256,4,4,128]{0,3,2,1:T(8,128)(2,1)S(1)}, bf16[256,512]{1,0:T(8,128)(2,1)S(1)}) %tuple.85), branch_computations={%region_4.5_spmd, %region_5.8_spmd} | conditional | flops 551043072 | bytes 34455604 | solution.py:67
  6.8 0.8 fusion.2
  8.3 1.3 copy-done
  9.5 1.8 fusion.4
  11.3 0.7 fusion.21
  12.1 5.3 %fusion.12 = f32[4,4,256,128]{3,2,1,0:T(8,128)} fusion(f32[4,256,256,4]{2,1,3,0:T(8,128)} %copy-done, f32[4,4,256]{2,1,0:T(4,128)} %get-tuple-element.380, pred[256,256]{0,1:T(8,128)(4,1)S(1)} %get-tuple-element.150, f32[4,4,256]{2,1,0:T(4,128)S(1)} %get-tuple-element.272, bf16[256,4,128,1]{2,1,0,3:T(4,128)(2,1)S(1)} %bitcast.78), kind=kOutput, calls=%fused_computation.12 | convolution fusion | flops 274202624 | bytes 6651904 | tf_op jit(solution)/shard_map/cond/branch_1_fun/hgqk,khd->hgqd/dot_general | solution.py:58
  17.4 157.6 %while.19 = (s32[]{:T(128)}, bf16[2,256,512]{1,2,0:T(8,128)(2,1)S(1)}, f32[4,4,256]{2,1,0:T(4,128)}, f32[4,4,256]{2,1,0:T(4,128)S(1)}, f32[4,4,256,128]{3,2,1,0:...) while((s32[]{:T(128)}, ...), condition=%wide.region_14.15_spmd.clone, body=%wide.region_8.14_spmd.clone.sunk | while | flops 551953152 | bytes 23076152 | solution.py:86
  17.4 3.8 %collective-permute-start = (bf16[2,256,512]{1,2,0:T(8,128)(2,1)S(1)}, bf16[2,256,512]{1,2,0:T(8,128)(2,1)S(1)}, u32[]{:S(2)}, u32[]{:S(2)}) collective-permute-start(bf16[2,256,512]{1,2,0:T(8,128)(2,1)S(1)} %get-tuple-element.396), channel_id=1, source_target_pairs={{0,4},{4,8},{8,12},{12,16},{16,20},{20,24},{24,28},{28,32},{32,36}... | collective-permute-start | bytes 1572872 | tf_op jit(solution)/shard_map/while/body/eval_jaxpr/ppermute | solution.py:15
  22.4 0.8 fusion.50
  23.8 3.4 %collective-permute-done = bf16[2,256,512]{1,2,0:T(8,128)(2,1)S(1)} collective-permute-done((bf16[2,256,512]{1,2,0:T(8,128)(2,1)S(1)}, bf16[2,256,512]{1,2,0:T(8,128)(2,1)S(1)}, u32[]{:S(2)}, u32[]{:S(2)}) %collective-permute-start) | collective-permute-done | bytes 524320 | tf_op jit(solution)/shard_map/while/body/eval_jaxpr/ppermute | solution.py:15
  27.2 8.1 %conditional.5 = ((f32[4,4,256]{2,1,0:T(4,128)}, f32[4,4,256]{2,1,0:T(4,128)S(1)}, f32[4,4,256,128]{3,2,1,0:T(8,128)})) conditional(s32[]{:T(128)} %convert_element_type.67, (f32[4,4,256]{2,1,0:T(4,128)}, f32[4,4,256]{2,1,0:T(4,128)S(1)}, f32[4,4,256,128]{3,2,1,0:T(8,128)}) %tuple.72, (pred[256,256]{0,1:T(8,128)(4,1)S(1)}, ...), branch_computations={%region_10.10_spmd, %region_11.13_spmd} | conditional | flops 551559168 | bytes 19857440 | solution.py:67
  27.3 0.9 fusion.22
  28.2 0.7 max.2
  28.9 1.0 fusion.24
  29.9 0.7 multiply_add_fusion.1
  30.7 4.1 %multiply_add_fusion = f32[4,4,256,128]{3,2,1,0:T(8,128)} fusion(f32[4,4,256,128]{3,2,1,0:T(8,128)} %get-tuple-element.159, bf16[256,4,128,1]{0,2,3,1:T(8,128)(2,1)S(1)} %bitcast.69, f32[4,256,256,4]{2,1,3,0:T(8,128)S(1)} %get-tuple-element.283, f32[4,4,256]{2,1,0:T(4,128)S(1)} %max.2, pred[256,256]{0,1:T(8,128)(4,1)S(1)} %get-tuple-element.155, ...), kind=kOutput, calls=%fused_computation.28 | convolution fusion | flops 274726912 | bytes 8749056 | tf_op jit(solution)/shard_map/while/body/eval_jaxpr/cond/branch_1_fun/hgqk,khd->hgqd/dot_general | solution.py:58
  35.4 4.4 %collective-permute-start = (bf16[2,256,512]{1,2,0:T(8,128)(2,1)S(1)}, bf16[2,256,512]{1,2,0:T(8,128)(2,1)S(1)}, u32[]{:S(2)}, u32[]{:S(2)}) collective-permute-start(bf16[2,256,512]{1,2,0:T(8,128)(2,1)S(1)} %get-tuple-element.396), channel_id=1, source_target_pairs={{0,4},{4,8},{8,12},{12,16},{16,20},{20,24},{24,28},{28,32},{32,36}... | collective-permute-start | bytes 1572872 | tf_op jit(solution)/shard_map/while/body/eval_jaxpr/ppermute | solution.py:15
  41.0 0.8 fusion.50
  42.5 3.4 %collective-permute-done = bf16[2,256,512]{1,2,0:T(8,128)(2,1)S(1)} collective-permute-done((bf16[2,256,512]{1,2,0:T(8,128)(2,1)S(1)}, bf16[2,256,512]{1,2,0:T(8,128)(2,1)S(1)}, u32[]{:S(2)}, u32[]{:S(2)}) %collective-permute-start) | collective-permute-done | bytes 524320 | tf_op jit(solution)/shard_map/while/body/eval_jaxpr/ppermute | solution.py:15
  45.9 4.4 %collective-permute-start = (bf16[2,256,512]{1,2,0:T(8,128)(2,1)S(1)}, bf16[2,256,512]{1,2,0:T(8,128)(2,1)S(1)}, u32[]{:S(2)}, u32[]{:S(2)}) collective-permute-start(bf16[2,256,512]{1,2,0:T(8,128)(2,1)S(1)} %get-tuple-element.396), channel_id=1, source_target_pairs={{0,4},{4,8},{8,12},{12,16},{16,20},{20,24},{24,28},{28,32},{32,36}... | collective-permute-start | bytes 1572872 | tf_op jit(solution)/shard_map/while/body/eval_jaxpr/ppermute | solution.py:15
  51.6 0.8 fusion.50
  53.0 12.2 %collective-permute-done = bf16[2,256,512]{1,2,0:T(8,128)(2,1)S(1)} collective-permute-done((bf16[2,256,512]{1,2,0:T(8,128)(2,1)S(1)}, bf16[2,256,512]{1,2,0:T(8,128)(2,1)S(1)}, u32[]{:S(2)}, u32[]{:S(2)}) %collective-permute-start) | collective-permute-done | bytes 524320 | tf_op jit(solution)/shard_map/while/body/eval_jaxpr/ppermute | solution.py:15
  65.3 1.9 collective-permute-start
  68.5 0.8 fusion.50
  69.9 17.3 %collective-permute-done = bf16[2,256,512]{1,2,0:T(8,128)(2,1)S(1)} collective-permute-done((bf16[2,256,512]{1,2,0:T(8,128)(2,1)S(1)}, bf16[2,256,512]{1,2,0:T(8,128)(2,1)S(1)}, u32[]{:S(2)}, u32[]{:S(2)}) %collective-permute-start) | collective-permute-done | bytes 524320 | tf_op jit(solution)/shard_map/while/body/eval_jaxpr/ppermute | solution.py:15
  87.2 1.9 collective-permute-start
  90.4 0.8 fusion.50
  91.9 17.3 %collective-permute-done = bf16[2,256,512]{1,2,0:T(8,128)(2,1)S(1)} collective-permute-done((bf16[2,256,512]{1,2,0:T(8,128)(2,1)S(1)}, bf16[2,256,512]{1,2,0:T(8,128)(2,1)S(1)}, u32[]{:S(2)}, u32[]{:S(2)}) %collective-permute-start) | collective-permute-done | bytes 524320 | tf_op jit(solution)/shard_map/while/body/eval_jaxpr/ppermute | solution.py:15
  109.2 1.9 collective-permute-start
  112.4 0.8 fusion.50
  113.8 17.3 %collective-permute-done = bf16[2,256,512]{1,2,0:T(8,128)(2,1)S(1)} collective-permute-done((bf16[2,256,512]{1,2,0:T(8,128)(2,1)S(1)}, bf16[2,256,512]{1,2,0:T(8,128)(2,1)S(1)}, u32[]{:S(2)}, u32[]{:S(2)}) %collective-permute-start) | collective-permute-done | bytes 524320 | tf_op jit(solution)/shard_map/while/body/eval_jaxpr/ppermute | solution.py:15
  131.1 1.9 collective-permute-start
  134.3 0.8 fusion.50
  135.8 17.3 %collective-permute-done = bf16[2,256,512]{1,2,0:T(8,128)(2,1)S(1)} collective-permute-done((bf16[2,256,512]{1,2,0:T(8,128)(2,1)S(1)}, bf16[2,256,512]{1,2,0:T(8,128)(2,1)S(1)}, u32[]{:S(2)}, u32[]{:S(2)}) %collective-permute-start) | collective-permute-done | bytes 524320 | tf_op jit(solution)/shard_map/while/body/eval_jaxpr/ppermute | solution.py:15
  153.1 1.9 collective-permute-start
  156.3 0.8 fusion.50
  157.7 17.3 %collective-permute-done = bf16[2,256,512]{1,2,0:T(8,128)(2,1)S(1)} collective-permute-done((bf16[2,256,512]{1,2,0:T(8,128)(2,1)S(1)}, bf16[2,256,512]{1,2,0:T(8,128)(2,1)S(1)}, u32[]{:S(2)}, u32[]{:S(2)}) %collective-permute-start) | collective-permute-done | bytes 524320 | tf_op jit(solution)/shard_map/while/body/eval_jaxpr/ppermute | solution.py:15
  175.0 1.9 copy.50
  177.2 20.7 %collective-permute-start.1 = (bf16[256,2048]{0,1:T(8,128)(2,1)S(1)}, bf16[256,2048]{0,1:T(8,128)(2,1)S(1)}, u32[]{:S(2)}, u32[]{:S(2)}) collective-permute-start(bf16[256,2048]{0,1:T(8,128)(2,1)S(1)} %bitcast.70), channel_id=1, source_target_pairs={{0,4},{4,0},{8,12},{12,8},{16,20},{20,16},{24,28},{28,24},{32,36},... | collective-permute-start | bytes 3145736 | tf_op jit(solution)/shard_map/ppermute | solution.py:25
  198.1 1.8 collective-permute-done.1
  200.3 2.5 %copy.51 = bf16[512,2048]{1,0:T(8,128)(2,1)} copy(bf16[512,2048]{0,1:T(8,128)(2,1)S(1)} %pad_maximum_fusion) | data formatting | bytes 4194304 | tf_op jit(solution)/shard_map/concatenate | solution.py:121
  202.8 3.2 %reshape.105 = bf16[4,262144]{1,0:T(4,128)(2,1)S(1)} reshape(bf16[512,2048]{1,0:T(8,128)(2,1)} %copy.51) | data formatting | bytes 4194304 | tf_op jit(solution)/shard_map/reshape | solution.py:121
  206.0 1.2 convolution_convert_fusion
  207.2 2.0 reshape.106
  (68 shorter events, 9.4 us)
Async XLA Ops:
  0.0 3.9 %copy-start.2 = (bf16[256,512]{1,0:T(8,128)(2,1)S(1)}, bf16[256,512]{1,0:T(8,128)(2,1)}, u32[]{:S(2)}) copy-start(bf16[256,512]{1,0:T(8,128)(2,1)} %param.12) | copy-start | bytes 786436
  0.0 4.1 %copy-start.1 = (bf16[256,512]{1,0:T(8,128)(2,1)S(1)}, bf16[256,512]{1,0:T(8,128)(2,1)}, u32[]{:S(2)}) copy-start(bf16[256,512]{1,0:T(8,128)(2,1)} %param.13) | copy-start | bytes 786436
  6.7 10.7 %copy-start.3 = (bf16[2,256,512]{1,2,0:T(8,128)(2,1)S(1)}, bf16[2,256,512]{1,2,0:T(8,128)(2,1)}, u32[]{:S(2)}) copy-start(bf16[2,256,512]{1,2,0:T(8,128)(2,1)} %pad_maximum_fusion.1) | copy-start | bytes 1572868
  7.6 1.9 copy-start
  17.4 9.9 %collective-permute-start = (bf16[2,256,512]{1,2,0:T(8,128)(2,1)S(1)}, bf16[2,256,512]{1,2,0:T(8,128)(2,1)S(1)}, u32[]{:S(2)}, u32[]{:S(2)}) collective-permute-start(bf16[2,256,512]{1,2,0:T(8,128)(2,1)S(1)} %get-tuple-element.396), channel_id=1, source_target_pairs={{0,4},{4,8},{8,12},{12,16},{16,20},{20,24},{24,28},{28,32},{32,36}... | collective-permute-start | bytes 1572872 | tf_op jit(solution)/shard_map/while/body/eval_jaxpr/ppermute | solution.py:15
  35.4 10.5 %collective-permute-start = (bf16[2,256,512]{1,2,0:T(8,128)(2,1)S(1)}, bf16[2,256,512]{1,2,0:T(8,128)(2,1)S(1)}, u32[]{:S(2)}, u32[]{:S(2)}) collective-permute-start(bf16[2,256,512]{1,2,0:T(8,128)(2,1)S(1)} %get-tuple-element.396), channel_id=1, source_target_pairs={{0,4},{4,8},{8,12},{12,16},{16,20},{20,24},{24,28},{28,32},{32,36}... | collective-permute-start | bytes 1572872 | tf_op jit(solution)/shard_map/while/body/eval_jaxpr/ppermute | solution.py:15
  45.9 19.3 %collective-permute-start = (bf16[2,256,512]{1,2,0:T(8,128)(2,1)S(1)}, bf16[2,256,512]{1,2,0:T(8,128)(2,1)S(1)}, u32[]{:S(2)}, u32[]{:S(2)}) collective-permute-start(bf16[2,256,512]{1,2,0:T(8,128)(2,1)S(1)} %get-tuple-element.396), channel_id=1, source_target_pairs={{0,4},{4,8},{8,12},{12,16},{16,20},{20,24},{24,28},{28,32},{32,36}... | collective-permute-start | bytes 1572872 | tf_op jit(solution)/shard_map/while/body/eval_jaxpr/ppermute | solution.py:15
  65.3 21.9 %collective-permute-start = (bf16[2,256,512]{1,2,0:T(8,128)(2,1)S(1)}, bf16[2,256,512]{1,2,0:T(8,128)(2,1)S(1)}, u32[]{:S(2)}, u32[]{:S(2)}) collective-permute-start(bf16[2,256,512]{1,2,0:T(8,128)(2,1)S(1)} %get-tuple-element.396), channel_id=1, source_target_pairs={{0,4},{4,8},{8,12},{12,16},{16,20},{20,24},{24,28},{28,32},{32,36}... | collective-permute-start | bytes 1572872 | tf_op jit(solution)/shard_map/while/body/eval_jaxpr/ppermute | solution.py:15
  87.2 21.9 %collective-permute-start = (bf16[2,256,512]{1,2,0:T(8,128)(2,1)S(1)}, bf16[2,256,512]{1,2,0:T(8,128)(2,1)S(1)}, u32[]{:S(2)}, u32[]{:S(2)}) collective-permute-start(bf16[2,256,512]{1,2,0:T(8,128)(2,1)S(1)} %get-tuple-element.396), channel_id=1, source_target_pairs={{0,4},{4,8},{8,12},{12,16},{16,20},{20,24},{24,28},{28,32},{32,36}... | collective-permute-start | bytes 1572872 | tf_op jit(solution)/shard_map/while/body/eval_jaxpr/ppermute | solution.py:15
  109.2 21.9 %collective-permute-start = (bf16[2,256,512]{1,2,0:T(8,128)(2,1)S(1)}, bf16[2,256,512]{1,2,0:T(8,128)(2,1)S(1)}, u32[]{:S(2)}, u32[]{:S(2)}) collective-permute-start(bf16[2,256,512]{1,2,0:T(8,128)(2,1)S(1)} %get-tuple-element.396), channel_id=1, source_target_pairs={{0,4},{4,8},{8,12},{12,16},{16,20},{20,24},{24,28},{28,32},{32,36}... | collective-permute-start | bytes 1572872 | tf_op jit(solution)/shard_map/while/body/eval_jaxpr/ppermute | solution.py:15
  131.1 21.9 %collective-permute-start = (bf16[2,256,512]{1,2,0:T(8,128)(2,1)S(1)}, bf16[2,256,512]{1,2,0:T(8,128)(2,1)S(1)}, u32[]{:S(2)}, u32[]{:S(2)}) collective-permute-start(bf16[2,256,512]{1,2,0:T(8,128)(2,1)S(1)} %get-tuple-element.396), channel_id=1, source_target_pairs={{0,4},{4,8},{8,12},{12,16},{16,20},{20,24},{24,28},{28,32},{32,36}... | collective-permute-start | bytes 1572872 | tf_op jit(solution)/shard_map/while/body/eval_jaxpr/ppermute | solution.py:15
  153.1 21.9 %collective-permute-start = (bf16[2,256,512]{1,2,0:T(8,128)(2,1)S(1)}, bf16[2,256,512]{1,2,0:T(8,128)(2,1)S(1)}, u32[]{:S(2)}, u32[]{:S(2)}) collective-permute-start(bf16[2,256,512]{1,2,0:T(8,128)(2,1)S(1)} %get-tuple-element.396), channel_id=1, source_target_pairs={{0,4},{4,8},{8,12},{12,16},{16,20},{20,24},{24,28},{28,32},{32,36}... | collective-permute-start | bytes 1572872 | tf_op jit(solution)/shard_map/while/body/eval_jaxpr/ppermute | solution.py:15
  175.0 22.9 %copy-start.4 = (s32[256]{0:T(256)S(1)}, s32[256]{0:T(256)}, u32[]{:S(2)}) copy-start(s32[256]{0:T(256)} %param.15) | copy-start | bytes 3076
  177.2 22.8 %collective-permute-start.1 = (bf16[256,2048]{0,1:T(8,128)(2,1)S(1)}, bf16[256,2048]{0,1:T(8,128)(2,1)S(1)}, u32[]{:S(2)}, u32[]{:S(2)}) collective-permute-start(bf16[256,2048]{0,1:T(8,128)(2,1)S(1)} %bitcast.70), channel_id=1, source_target_pairs={{0,4},{4,0},{8,12},{12,8},{16,20},{20,16},{24,28},{28,24},{32,36},... | collective-permute-start | bytes 3145736 | tf_op jit(solution)/shard_map/ppermute | solution.py:25
where the time goes:
time: 212 us; the launch traced here: 209 us
  waiting for transfers between devices  107 us (50%)
  starting transfers between devices  42.8 us (20%)
  local copies, waits for them, and re-layouts  19.8 us (9%)
  other arithmetic  15.5 us (7%)
  matrix products  12.3 us (6%)
  loops' own time  10.8 us (5%)
    ppermute x8, waiting for transfers between devices, shifted(): lax.ppermute(value, axis, [(source, source + steps) for source in range(i...  105 us
    ppermute x8, starting transfers between devices, shifted(): lax.ppermute(value, axis, [(source, source + steps) for source in range(i...  22.1 us
    ppermute x1, starting transfers between devices, partner_2(): return lax.ppermute(block, axis, route)  20.7 us
    another operation x1, loops' own time, context_fold(): lax.scan(advance, (key_values, softmax_state), jnp.arange(1, depth + 1, d...  10.8 us
    dot_general x2, matrix products, update(): jnp.einsum('hgqk,khd->hgqd', weights.astype(jnp.bfloat16), value_rows, pr...  9.32 us
    reduce_or x8, other arithmetic, fold_piece(): jnp.any(allowed)  6.23 us
    dynamic_slice x8, local copies, waits for them, and re-layouts, context_fold(): lax.scan(advance, (key_values, softmax_state), jnp.arange(1, depth + 1, d...  4.71 us
  transfers between devices with their start and end apart: 9, of which 9 were waited for; matrix products, arithmetic and copies ran while one was open for 5% of the time, Pallas kernels for 0%

commit v1 on v0

v1 whole, which is shorter than its diff:
```python
import functools
import math

import jax
import jax.numpy as jnp
from jax import lax
from jax.experimental import pallas as pl
from jax.experimental.pallas import tpu as pltpu
from jax.sharding import PartitionSpec as P

HD = 128
BLOCK = 128
WINDOW = 2048
ROWS = 256
HEADS = 8
HALF = HEADS * HD
LOG2E = math.log2(math.e)
FACTOR = HD**-0.5 * LOG2E
NEG = -1e30
VLIM = 48 * 1024 * 1024


def vmem(shape, dtype):
    return pltpu.VMEM(shape, dtype)


def params():
    return pltpu.CompilerParams(vmem_limit_bytes=VLIM)


VSPEC = pl.BlockSpec(memory_space=pltpu.VMEM)
SSPEC = pl.BlockSpec(memory_space=pltpu.SMEM)


def pack_kernel(meta, q, k, v, near, cross, swap):
    core = meta[0]
    other = 1 - core
    mine = pl.ds(pl.multiple_of(core * 256, 256), 256)
    theirs = pl.ds(pl.multiple_of(other * 256, 256), 256)
    near[:, 0:256] = k[:, mine]
    near[:, 256:512] = v[:, mine]
    k_other = k[:, theirs]
    v_other = v[:, theirs]
    cross[:, 0:256] = k_other
    cross[:, 256:512] = v_other
    swap[:, 0:HALF] = q[:, pl.ds(pl.multiple_of(other * HALF, HALF), HALF)]
    swap[:, HALF : HALF + 256] = k_other
    swap[:, HALF + 256 : HALF + 512] = v_other


def tile_update(q, kv, k_col, lo, key_pos_base, row_pos, row, acc, top, low, first, masked):
    rows = pl.ds(pl.multiple_of(row, BLOCK), BLOCK)
    if masked:
        key_pos = key_pos_base + lax.broadcasted_iota(jnp.int32, (BLOCK, ROWS), 1)
        last = row_pos + lax.broadcasted_iota(jnp.int32, (BLOCK, ROWS), 0)
        allowed = (key_pos <= last) & (key_pos >= lo[rows, :])
        bias = jnp.where(allowed, jnp.float32(0.0), jnp.float32(NEG))
    for head in range(HEADS):
        cols = pl.ds(head * HD, HD)
        kvh = head // 4
        keys = kv[:, k_col + kvh * HD : k_col + (kvh + 1) * HD]
        vals = kv[:, k_col + 256 + kvh * HD : k_col + 256 + (kvh + 1) * HD]
        s = lax.dot_general(
            q[rows, cols], keys, (((1,), (1,)), ((), ())), preferred_element_type=jnp.float32
        )
        if masked:
            s = s + bias
        peak = jnp.max(jnp.maximum(s[:, :HD], s[:, HD:]), axis=1, keepdims=True)
        if first:
            new_top = jnp.broadcast_to(peak, (BLOCK, HD))
        else:
            old_top = top[rows, cols]
            new_top = jnp.maximum(old_top, peak)
            keep = jnp.exp2((old_top - new_top) * FACTOR)
        shift = new_top * FACTOR
        p0 = jnp.exp2(s[:, :HD] * FACTOR - shift)
        p1 = jnp.exp2(s[:, HD:] * FACTOR - shift)
        p = jnp.concatenate([p0, p1], axis=1).astype(jnp.bfloat16)
        mixed = jnp.dot(p, vals, preferred_element_type=jnp.float32)
        part = p0 + p1
        top[rows, cols] = new_top
        if first:
            low[rows, cols] = part
            acc[rows, cols] = mixed
        else:
            low[rows, cols] = low[rows, cols] * keep + part
            acc[rows, cols] = acc[rows, cols] * keep + mixed


def chunk_update(meta, q, kv, k_col, lo, key_base, acc, top, low, blocks):
    def body(block, carry):
        row = block * BLOCK
        row_pos = meta[1 + block]
        lo_first = meta[5 + block]
        lo_last = meta[9 + block]
        some = (key_base <= row_pos + BLOCK - 1) & (key_base + ROWS - 1 >= lo_first)
        full = (key_base + ROWS - 1 <= row_pos) & (key_base >= lo_last)
        args = (q, kv, k_col, lo, key_base, row_pos, row, acc, top, low, False)

        @pl.when(full)
        def _():
            tile_update(*args, False)

        @pl.when(some & jnp.logical_not(full))
        def _():
            tile_update(*args, True)

        return carry

    lax.fori_loop(blocks[0], blocks[1], body, 0)


def first_kernel(meta, lo, q, near, recv, qcat, acc, top, low):
    core = meta[0]
    qcat[0:ROWS, :] = q[:, pl.ds(pl.multiple_of(core * HALF, HALF), HALF)]
    qcat[ROWS : 2 * ROWS, :] = recv[:, 0:HALF]
    own_base = meta[1]
    far_base = meta[3]
    for kv, col, base, start in ((near, 0, own_base, 0), (recv, HALF, far_base, 2)):

        def body(block, carry, kv=kv, col=col, base=base):
            tile_update(
                qcat, kv, col, lo, base, meta[1 + block], block * BLOCK, acc, top, low, True, True
            )
            return carry

        lax.fori_loop(start, start + 2, body, 0)
    chunk_update(meta, qcat, recv, HALF, lo, far_base, acc, top, low, (0, 2))
    chunk_update(meta, qcat, near, 0, lo, own_base, acc, top, low, (2, 4))


def next_kernel(step, cross, meta, lo, q, kv, acc_in, top_in, low_in, acc, top, low):
    base = meta[3 if cross else 1] - step * 2 * ROWS
    chunk_update(meta, q, kv, 0, lo, base, acc, top, low, (0, 4))


def last_kernel(step, cross, meta, lo, q, kv, acc_in, top_in, low_in, keep, send, acc, top, low):
    next_kernel(step, cross, meta, lo, q, kv, acc_in, top_in, low_in, acc, top, low)

    def body(block, carry):
        rows = pl.ds(pl.multiple_of(block * BLOCK, BLOCK), BLOCK)
        slot = pl.ds(pl.multiple_of(meta[17 + block] * BLOCK, BLOCK), BLOCK)

        def write(ref):
            for head in range(HEADS):
                cols = pl.ds(head * HD, HD)
                total = jnp.sum(low[rows, cols], axis=1, keepdims=True)
                ref[slot, cols] = (acc[rows, cols] / total).astype(jnp.bfloat16)

        @pl.when(meta[13 + block] == 1)
        def _():
            write(keep)

        @pl.when(meta[13 + block] == 0)
        def _():
            write(send)

        return carry

    lax.fori_loop(0, 4, body, 0)


def join_kernel(meta, keep, recv, out):
    core = meta[0]
    mine = pl.ds(pl.multiple_of(core * HALF, HALF), HALF)
    theirs = pl.ds(pl.multiple_of((1 - core) * HALF, HALF), HALF)
    out[:, mine] = keep[...]
    out[:, theirs] = recv[...]


STATE = [vmem((2 * ROWS, HALF), jnp.float32)] * 3


def cost(tiles):
    return pl.CostEstimate(
        flops=tiles * 4 * ROWS * ROWS * HD * HEADS,
        bytes_accessed=1 << 20,
        transcendentals=tiles * ROWS * ROWS * HEADS,
    )


def local(queries, keys, values, lengths, home):
    device = lax.axis_index("seq")
    count = lax.axis_size("seq")
    core = device % 2
    partner = device + 1 - 2 * core
    docs = lengths.shape[0]
    order = jnp.arange(docs, dtype=jnp.int32)
    starts = jnp.sum(jnp.where(order[None, :] < order[:, None], lengths[None, :], 0), axis=1)
    block_pos = jnp.stack(
        [device * ROWS, device * ROWS + BLOCK, partner * ROWS, partner * ROWS + BLOCK]
    ).astype(jnp.int32)
    row_pos = (block_pos[:, None] + jnp.arange(BLOCK, dtype=jnp.int32)[None, :]).reshape(-1)
    doc_first = jnp.max(jnp.where(starts[None, :] <= row_pos[:, None], starts[None, :], 0), axis=1)
    lo = jnp.maximum(doc_first, row_pos - (WINDOW - 1))
    by_block = lo.reshape(4, BLOCK)
    base_block = (device - core) * 2
    group_home = lax.dynamic_slice_in_dim(home, base_block, 4, 0)
    ranks = jnp.sum(
        (group_home[None, :] == group_home[:, None])
        & (jnp.arange(4)[None, :] < jnp.arange(4)[:, None]),
        axis=1,
    ).astype(jnp.int32)
    mine = (group_home == device).astype(jnp.int32)
    turn = jnp.where(core == 0, jnp.arange(4), (jnp.arange(4) + 2) % 4)
    pick = (turn[:, None] == jnp.arange(4)[None, :]).astype(jnp.int32)
    meta = jnp.concatenate(
        [
            core[None].astype(jnp.int32),
            block_pos,
            by_block[:, 0],
            by_block[:, -1],
            jnp.sum(pick * mine[None, :], axis=1),
            jnp.sum(pick * ranks[None, :], axis=1),
        ]
    ).astype(jnp.int32)
    lo = lo[:, None]

    near, cross, swap = pl.pallas_call(
        pack_kernel,
        out_shape=[
            vmem((ROWS, 512), jnp.bfloat16),
            vmem((ROWS, 512), jnp.bfloat16),
            vmem((ROWS, HALF + 512), jnp.bfloat16),
        ],
        in_specs=[SSPEC] + [VSPEC] * 3,
        out_specs=[VSPEC] * 3,
        compiler_params=params(),
        name="pack",
    )(core[None].astype(jnp.int32), queries, keys, values)

    same = [(i, i + 2) for i in range(count - 2)]
    other = [(i, (i ^ 1) + 2) for i in range(count - 2)]
    pair = [(i, i ^ 1) for i in range(count)]
    shift = functools.partial(lax.ppermute, axis_name="seq")
    chunks = [[shift(near, perm=same)], [shift(cross, perm=other)]]
    recv = shift(swap, perm=pair)
    for step in range(1, 4):
        for chain in chunks:
            chain.append(shift(chain[-1], perm=same))

    qcat, *state = pl.pallas_call(
        first_kernel,
        out_shape=[vmem((2 * ROWS, HALF), jnp.bfloat16)] + STATE,
        in_specs=[SSPEC] + [VSPEC] * 4,
        out_specs=[VSPEC] * 4,
        compiler_params=params(),
        cost_estimate=cost(3),
        name="first",
    )(meta, lo, queries, near, recv)
    for step in range(4):
        for side in range(2):
            last = step == 3 and side == 1
            kernel = last_kernel if last else next_kernel
            extra = [vmem((ROWS, HALF), jnp.bfloat16)] * 2 if last else []
            kv = chunks[side][step]
            results = pl.pallas_call(
                functools.partial(kernel, step + 1, side == 1),
                out_shape=extra + STATE,
                in_specs=[SSPEC] + [VSPEC] * 6,
                out_specs=[VSPEC] * (3 + len(extra)),
                input_output_aliases={4: len(extra), 5: len(extra) + 1, 6: len(extra) + 2},
                compiler_params=params(),
                cost_estimate=cost(2),
                name="last" if last else "next",
            )(meta, lo, qcat, kv, *state)
            state = results[len(extra) :]
    keep, send = results[:2]
    got = shift(send, perm=pair)
    return pl.pallas_call(
        join_kernel,
        out_shape=jax.ShapeDtypeStruct((ROWS, 2 * HALF), jnp.bfloat16),
        in_specs=[SSPEC] + [VSPEC] * 2,
        out_specs=VSPEC,
        compiler_params=params(),
        name="join",
    )(core[None].astype(jnp.int32), keep, got)


def solution(mesh):
    placed = (
        P(("pack", "seq"), None),
        P(("pack", "seq"), None),
        P(("pack", "seq"), None),
        P("pack"),
        P("pack"),
    )
    return jax.shard_map(
        local, mesh=mesh, in_specs=placed, out_specs=P(("pack", "seq"), None), check_vma=False
    )
```

time: 212 us -> 104 us (0.49)
  the two profiles are of different devices: /device:TPU:263 before, /device:TPU:441 now
where the time goes in v1:
time: 104 us
  Pallas kernels  46.3 us (45%)
  starting transfers between devices  37.3 us (36%)
  waiting for transfers between devices  10 us (10%)
  local copies, waits for them, and re-layouts  6.63 us (6%)
  other arithmetic  3.09 us (3%)
    pallas_call x8, Pallas kernels, local(): pl.pallas_call(functools.partial(kernel, step + 1, side == 1), out_shape=...  38.4 us
    ppermute x6, starting transfers between devices, local(): chain.append(shift(chain[-1], perm=same))  23 us
    pallas_call x1, Pallas kernels, local(): pl.pallas_call(first_kernel, out_shape=[vmem((2 * ROWS, HALF), jnp.bfloat...  6.79 us
    ppermute x1, starting transfers between devices, local(): got = shift(send, perm=pair)  6.04 us
    ppermute x2, starting transfers between devices, local(): chunks = [[shift(near, perm=same)], [shift(cross, perm=other)]]  5.69 us
    unnamed x26, local copies, waits for them, and re-layouts  5.49 us
    ppermute x2, waiting for transfers between devices, local(): chunks = [[shift(near, perm=same)], [shift(cross, perm=other)]]  4.65 us
    ppermute x6, waiting for transfers between devices, local(): chain.append(shift(chain[-1], perm=same))  3.85 us
  transfers between devices with their start and end apart: 10, of which 6 were waited for; matrix products, arithmetic and copies ran while one was open for 4% of the time, Pallas kernels for 40%

profile of v1, /device:TPU:441, one launch (start us, length us, event | category | flops | bytes accessed | tf_op | source)
XLA Modules:
  0.0 103.7 jit_solution(11161945095968098668)
XLA Ops:
  0.0 1.2 %copy-done.1 = bf16[256,2048]{1,0:T(8,128)(2,1)S(1)} copy-done((bf16[256,2048]{1,0:T(8,128)(2,1)S(1)}, bf16[256,2048]{1,0:T(8,128)(2,1)}, u32[]{:S(2)}) %copy-start.1) | copy-done | bytes 1048600
  1.2 0.9 copy-done.2
  2.2 0.9 copy-done.3
  3.1 0.1 pack.1
  3.2 0.0 copy-start.4
  3.2 2.6 %collective-permute-start = (bf16[256,1536]{1,0:T(8,128)(2,1)S(1)}, bf16[256,1536]{1,0:T(8,128)(2,1)}, u32[]{:S(2)}, u32[]{:S(2)}) collective-permute-start(bf16[256,1536]{1,0:T(8,128)(2,1)S(1)} %get-tuple-element.36), channel_id=1, source_target_pairs={{0,4},{4,0},{8,12},{12,8},{16,20},{20,16},{24,28},{28,24},{32,36},... | collective-permute-start | bytes 2359304 | tf_op jit(solution)/shard_map/ppermute | solution.py:237
  5.8 2.3 %collective-permute-start.5 = (bf16[256,512]{1,0:T(8,128)(2,1)S(1)}, bf16[256,512]{1,0:T(8,128)(2,1)S(1)}, u32[]{:S(2)}, u32[]{:S(2)}) collective-permute-start(bf16[256,512]{1,0:T(8,128)(2,1)S(1)} %get-tuple-element.35.near), channel_id=1, source_target_pairs={{0,8},{4,12},{8,16},{12,20},{16,24},{20,28},{24,32},{28,36},{32,40... | collective-permute-start | bytes 786440 | tf_op jit(solution)/shard_map/ppermute | solution.py:236
  8.1 3.4 %collective-permute-start.1 = (bf16[256,512]{1,0:T(8,128)(2,1)S(1)}, bf16[256,512]{1,0:T(8,128)(2,1)S(1)}, u32[]{:S(2)}, u32[]{:S(2)}) collective-permute-start(bf16[256,512]{1,0:T(8,128)(2,1)S(1)} %get-tuple-element.38), channel_id=1, source_target_pairs={{0,12},{4,8},{8,20},{12,16},{16,28},{20,24},{24,36},{28,32},{32,44... | collective-permute-start | bytes 786440 | tf_op jit(solution)/shard_map/ppermute | solution.py:236
  11.5 0.1 pad_add_fusion
  11.6 0.1 fusion.1
  11.7 0.8 select_reduce_fusion.1
  12.5 0.2 select_reduce_fusion
  12.7 2.9 %collective-permute-done.5.kv = bf16[256,512]{1,0:T(8,128)(2,1)S(1)} collective-permute-done((bf16[256,512]{1,0:T(8,128)(2,1)S(1)}, bf16[256,512]{1,0:T(8,128)(2,1)S(1)}, u32[]{:S(2)}, u32[]{:S(2)}) %collective-permute-start.5) | collective-permute-done | bytes 262176 | tf_op jit(solution)/shard_map/ppermute | solution.py:236
  15.7 4.4 %collective-permute-start.6 = (bf16[256,512]{1,0:T(8,128)(2,1)S(1)}, bf16[256,512]{1,0:T(8,128)(2,1)S(1)}, u32[]{:S(2)}, u32[]{:S(2)}) collective-permute-start(bf16[256,512]{1,0:T(8,128)(2,1)S(1)} %collective-permute-done.5.kv), channel_id=1, source_target_pairs={{0,8},{4,12},{8,16},{12,20},{16,24},{20,28},{24,32},{28,36},{32,40... | collective-permute-start | bytes 786440 | tf_op jit(solution)/shard_map/ppermute | solution.py:240
  20.1 1.7 %collective-permute-done.1.kv = bf16[256,512]{1,0:T(8,128)(2,1)S(1)} collective-permute-done((bf16[256,512]{1,0:T(8,128)(2,1)S(1)}, bf16[256,512]{1,0:T(8,128)(2,1)S(1)}, u32[]{:S(2)}, u32[]{:S(2)}) %collective-permute-start.1) | collective-permute-done | bytes 262176 | tf_op jit(solution)/shard_map/ppermute | solution.py:236
  21.8 4.0 %collective-permute-start.2 = (bf16[256,512]{1,0:T(8,128)(2,1)S(1)}, bf16[256,512]{1,0:T(8,128)(2,1)S(1)}, u32[]{:S(2)}, u32[]{:S(2)}) collective-permute-start(bf16[256,512]{1,0:T(8,128)(2,1)S(1)} %collective-permute-done.1.kv), channel_id=1, source_target_pairs={{0,8},{4,12},{8,16},{12,20},{16,24},{20,28},{24,32},{28,36},{32,40... | collective-permute-start | bytes 786440 | tf_op jit(solution)/shard_map/ppermute | solution.py:240
  25.8 0.1 fusion
  25.9 0.8 compare_convert_fusion
  26.6 0.2 slice_reduce_fusion
  26.8 0.1 collective-permute-done.6.kv
  26.9 3.8 %collective-permute-start.7 = (bf16[256,512]{1,0:T(8,128)(2,1)S(1)}, bf16[256,512]{1,0:T(8,128)(2,1)S(1)}, u32[]{:S(2)}, u32[]{:S(2)}) collective-permute-start(bf16[256,512]{1,0:T(8,128)(2,1)S(1)} %collective-permute-done.6.kv), channel_id=1, source_target_pairs={{0,8},{4,12},{8,16},{12,20},{16,24},{20,28},{24,32},{28,36},{32,40... | collective-permute-start | bytes 786440 | tf_op jit(solution)/shard_map/ppermute | solution.py:240
  30.7 1.8 %collective-permute-done.2.kv = bf16[256,512]{1,0:T(8,128)(2,1)S(1)} collective-permute-done((bf16[256,512]{1,0:T(8,128)(2,1)S(1)}, bf16[256,512]{1,0:T(8,128)(2,1)S(1)}, u32[]{:S(2)}, u32[]{:S(2)}) %collective-permute-start.2) | collective-permute-done | bytes 262176 | tf_op jit(solution)/shard_map/ppermute | solution.py:240
  32.5 4.9 %collective-permute-start.3 = (bf16[256,512]{1,0:T(8,128)(2,1)S(1)}, bf16[256,512]{1,0:T(8,128)(2,1)S(1)}, u32[]{:S(2)}, u32[]{:S(2)}) collective-permute-start(bf16[256,512]{1,0:T(8,128)(2,1)S(1)} %collective-permute-done.2.kv), channel_id=1, source_target_pairs={{0,8},{4,12},{8,16},{12,20},{16,24},{20,28},{24,32},{28,36},{32,40... | collective-permute-start | bytes 786440 | tf_op jit(solution)/shard_map/ppermute | solution.py:240
  37.4 0.1 copy.36
  37.6 0.1 copy.35
  37.7 0.7 max.14.lo
  38.5 0.2 convert_reduce_fusion
  38.6 0.2 select_reduce_fusion.2
  38.8 0.7 concatenate.4.meta
  39.5 2.3 %collective-permute-start.8 = (bf16[256,512]{1,0:T(8,128)(2,1)S(1)}, bf16[256,512]{1,0:T(8,128)(2,1)S(1)}, u32[]{:S(2)}, u32[]{:S(2)}) collective-permute-start(bf16[256,512]{1,0:T(8,128)(2,1)S(1)} %collective-permute-done.7.kv), channel_id=1, source_target_pairs={{0,8},{4,12},{8,16},{12,20},{16,24},{20,28},{24,32},{28,36},{32,40... | collective-permute-start | bytes 786440 | tf_op jit(solution)/shard_map/ppermute | solution.py:240
  41.8 1.9 %collective-permute-done.3.kv = bf16[256,512]{1,0:T(8,128)(2,1)S(1)} collective-permute-done((bf16[256,512]{1,0:T(8,128)(2,1)S(1)}, bf16[256,512]{1,0:T(8,128)(2,1)S(1)}, u32[]{:S(2)}, u32[]{:S(2)}) %collective-permute-start.3) | collective-permute-done | bytes 262176 | tf_op jit(solution)/shard_map/ppermute | solution.py:240
  43.7 3.6 %collective-permute-start.4 = (bf16[256,512]{1,0:T(8,128)(2,1)S(1)}, bf16[256,512]{1,0:T(8,128)(2,1)S(1)}, u32[]{:S(2)}, u32[]{:S(2)}) collective-permute-start(bf16[256,512]{1,0:T(8,128)(2,1)S(1)} %collective-permute-done.3.kv), channel_id=1, source_target_pairs={{0,8},{4,12},{8,16},{12,20},{16,24},{20,28},{24,32},{28,36},{32,40... | collective-permute-start | bytes 786440 | tf_op jit(solution)/shard_map/ppermute | solution.py:240
  47.4 6.8 %first.1 = (bf16[512,1024]{1,0:T(8,128)(2,1)S(1)}, f32[512,1024]{1,0:T(8,128)S(1)}, f32[512,1024]{1,0:T(8,128)S(1)}, f32[512,1024]{1,0:T(8,128)S(1)}) custom-call(s32[21]{0:T(128)} %concatenate.4.meta, s32[512,1]{1,0:T(8,128)} %max.14.lo, bf16[256,2048]{1,0:T(8,128)(2,1)} %q.3, bf16[256,512]{1,0:T(8,128)(2,1)} %copy-done.4, ...), custom_call_target="tpu_custom_call" | custom-call | flops 805306368 | bytes 1048576 | tf_op jit(solution)/shard_map/first/pallas_call | solution.py:242
  54.2 0.0 copy-start
  54.2 1.0 copy-done
  55.2 4.9 %next.7 = (f32[512,1024]{1,0:T(8,128)S(1)}, f32[512,1024]{1,0:T(8,128)S(1)}, f32[512,1024]{1,0:T(8,128)S(1)}) custom-call(s32[21]{0:T(128)} %concatenate.4.meta, s32[512,1]{1,0:T(8,128)} %max.14.lo, bf16[512,1024]{1,0:T(8,128)(2,1)} %copy-done, bf16[256,512]{1,0:T(8,128)(2,1)} %copy-done.6, ...), custom_call_target="tpu_custom_call", output_to_operand_aliasing={{0}: (4, {}), {1}: (5, {}), {2}: (6, {})} | custom-call | flops 536870912 | bytes 1048576 | tf_op jit(solution)/shard_map/next/pallas_call | solution.py:257
  60.1 4.9 %next.8 = (f32[512,1024]{1,0:T(8,128)S(1)}, f32[512,1024]{1,0:T(8,128)S(1)}, f32[512,1024]{1,0:T(8,128)S(1)}) custom-call(s32[21]{0:T(128)} %concatenate.4.meta, s32[512,1]{1,0:T(8,128)} %max.14.lo, bf16[512,1024]{1,0:T(8,128)(2,1)} %copy-done, bf16[256,512]{1,0:T(8,128)(2,1)} %copy-done.5, ...), custom_call_target="tpu_custom_call", output_to_operand_aliasing={{0}: (4, {}), {1}: (5, {}), {2}: (6, {})} | custom-call | flops 536870912 | bytes 1048576 | tf_op jit(solution)/shard_map/next/pallas_call | solution.py:257
  65.0 4.9 %next.9 = (f32[512,1024]{1,0:T(8,128)S(1)}, f32[512,1024]{1,0:T(8,128)S(1)}, f32[512,1024]{1,0:T(8,128)S(1)}) custom-call(s32[21]{0:T(128)} %concatenate.4.meta, s32[512,1]{1,0:T(8,128)} %max.14.lo, bf16[512,1024]{1,0:T(8,128)(2,1)} %copy-done, bf16[256,512]{1,0:T(8,128)(2,1)} %copy-done.8, ...), custom_call_target="tpu_custom_call", output_to_operand_aliasing={{0}: (4, {}), {1}: (5, {}), {2}: (6, {})} | custom-call | flops 536870912 | bytes 1048576 | tf_op jit(solution)/shard_map/next/pallas_call | solution.py:257
  69.8 4.9 %next.10 = (f32[512,1024]{1,0:T(8,128)S(1)}, f32[512,1024]{1,0:T(8,128)S(1)}, f32[512,1024]{1,0:T(8,128)S(1)}) custom-call(s32[21]{0:T(128)} %concatenate.4.meta, s32[512,1]{1,0:T(8,128)} %max.14.lo, bf16[512,1024]{1,0:T(8,128)(2,1)} %copy-done, bf16[256,512]{1,0:T(8,128)(2,1)} %copy-done.7, ...), custom_call_target="tpu_custom_call", output_to_operand_aliasing={{0}: (4, {}), {1}: (5, {}), {2}: (6, {})} | custom-call | flops 536870912 | bytes 1048576 | tf_op jit(solution)/shard_map/next/pallas_call | solution.py:257
  74.7 4.9 %next.11 = (f32[512,1024]{1,0:T(8,128)S(1)}, f32[512,1024]{1,0:T(8,128)S(1)}, f32[512,1024]{1,0:T(8,128)S(1)}) custom-call(s32[21]{0:T(128)} %concatenate.4.meta, s32[512,1]{1,0:T(8,128)} %max.14.lo, bf16[512,1024]{1,0:T(8,128)(2,1)} %copy-done, bf16[256,512]{1,0:T(8,128)(2,1)} %copy-done.10, ...), custom_call_target="tpu_custom_call", output_to_operand_aliasing={{0}: (4, {}), {1}: (5, {}), {2}: (6, {})} | custom-call | flops 536870912 | bytes 1048576 | tf_op jit(solution)/shard_map/next/pallas_call | solution.py:257
  79.6 5.0 %next.12 = (f32[512,1024]{1,0:T(8,128)S(1)}, f32[512,1024]{1,0:T(8,128)S(1)}, f32[512,1024]{1,0:T(8,128)S(1)}) custom-call(s32[21]{0:T(128)} %concatenate.4.meta, s32[512,1]{1,0:T(8,128)} %max.14.lo, bf16[512,1024]{1,0:T(8,128)(2,1)} %copy-done, bf16[256,512]{1,0:T(8,128)(2,1)} %copy-done.9, ...), custom_call_target="tpu_custom_call", output_to_operand_aliasing={{0}: (4, {}), {1}: (5, {}), {2}: (6, {})} | custom-call | flops 536870912 | bytes 1048576 | tf_op jit(solution)/shard_map/next/pallas_call | solution.py:257
  84.6 0.7 copy-done.12
  85.3 4.9 %next.13 = (f32[512,1024]{1,0:T(8,128)S(1)}, f32[512,1024]{1,0:T(8,128)S(1)}, f32[512,1024]{1,0:T(8,128)S(1)}) custom-call(s32[21]{0:T(128)} %concatenate.4.meta, s32[512,1]{1,0:T(8,128)} %max.14.lo, bf16[512,1024]{1,0:T(8,128)(2,1)} %copy-done, bf16[256,512]{1,0:T(8,128)(2,1)} %copy-done.12, ...), custom_call_target="tpu_custom_call", output_to_operand_aliasing={{0}: (4, {}), {1}: (5, {}), {2}: (6, {})} | custom-call | flops 536870912 | bytes 1048576 | tf_op jit(solution)/shard_map/next/pallas_call | solution.py:257
  90.2 0.7 copy-done.11
  90.9 4.1 %last.1 = (bf16[256,1024]{1,0:T(8,128)(2,1)S(1)}, bf16[256,1024]{1,0:T(8,128)(2,1)S(1)}, f32[512,1024]{1,0:T(8,128)S(1)}, f32[512,1024]{1,0:T(8,128)S(1)}, f32[512,1024]{1,0:T(8,128)S(1)}) custom-call(s32[21]{0:T(128)} %concatenate.4.meta, s32[512,1]{1,0:T(8,128)} %max.14.lo, ...), custom_call_target="tpu_custom_call", output_to_operand_aliasing={{2}: (4, {}), {3}: (5, {}), {4}: (6, {})} | custom-call | flops 536870912 | bytes 1048576 | tf_op jit(solution)/shard_map/last/pallas_call | solution.py:257
  95.1 6.0 %collective-permute-start.9 = (bf16[256,1024]{1,0:T(8,128)(2,1)S(1)}, bf16[256,1024]{1,0:T(8,128)(2,1)S(1)}, u32[]{:S(2)}, u32[]{:S(2)}) collective-permute-start(bf16[256,1024]{1,0:T(8,128)(2,1)S(1)} %get-tuple-element.64), channel_id=1, source_target_pairs={{0,4},{4,0},{8,12},{12,8},{16,20},{20,16},{24,28},{28,24},{32,36},... | collective-permute-start | bytes 1572872 | tf_op jit(solution)/shard_map/ppermute | solution.py:269
  101.1 1.5 %collective-permute-done.9.recv = bf16[256,1024]{1,0:T(8,128)(2,1)S(1)} collective-permute-done((bf16[256,1024]{1,0:T(8,128)(2,1)S(1)}, bf16[256,1024]{1,0:T(8,128)(2,1)S(1)}, u32[]{:S(2)}, u32[]{:S(2)}) %collective-permute-start.9) | collective-permute-done | bytes 524320 | tf_op jit(solution)/shard_map/ppermute | solution.py:269
  102.6 1.0 %join.1 = bf16[256,2048]{1,0:T(8,128)(2,1)} custom-call(s32[1]{0:T(128)} %bitcast.meta, bf16[256,1024]{1,0:T(8,128)(2,1)S(1)} %get-tuple-element.63.keep, bf16[256,1024]{1,0:T(8,128)(2,1)S(1)} %collective-permute-done.9.recv), custom_call_target="tpu_custom_call" | custom-call | tf_op jit(solution)/shard_map/join/pallas_call | solution.py:270
  (23 shorter events, 0.0 us)
Async XLA Ops:
  0.0 1.2 %copy-start.1 = (bf16[256,2048]{1,0:T(8,128)(2,1)S(1)}, bf16[256,2048]{1,0:T(8,128)(2,1)}, u32[]{:S(2)}) copy-start(bf16[256,2048]{1,0:T(8,128)(2,1)} %q.3) | copy-start | bytes 3145732
  1.2 0.9 copy-start.2
  2.2 0.9 copy-start.3
  3.2 44.2 %copy-start.4 = (bf16[256,512]{1,0:T(8,128)(2,1)}, bf16[256,512]{1,0:T(8,128)(2,1)S(1)}, u32[]{:S(2)}) copy-start(bf16[256,512]{1,0:T(8,128)(2,1)S(1)} %get-tuple-element.35.near) | copy-start | bytes 786436
  3.2 44.1 %collective-permute-start = (bf16[256,1536]{1,0:T(8,128)(2,1)S(1)}, bf16[256,1536]{1,0:T(8,128)(2,1)}, u32[]{:S(2)}, u32[]{:S(2)}) collective-permute-start(bf16[256,1536]{1,0:T(8,128)(2,1)S(1)} %get-tuple-element.36), channel_id=1, source_target_pairs={{0,4},{4,0},{8,12},{12,8},{16,20},{20,16},{24,28},{28,24},{32,36},... | collective-permute-start | bytes 2359304 | tf_op jit(solution)/shard_map/ppermute | solution.py:237
  5.8 9.8 %collective-permute-start.5 = (bf16[256,512]{1,0:T(8,128)(2,1)S(1)}, bf16[256,512]{1,0:T(8,128)(2,1)S(1)}, u32[]{:S(2)}, u32[]{:S(2)}) collective-permute-start(bf16[256,512]{1,0:T(8,128)(2,1)S(1)} %get-tuple-element.35.near), channel_id=1, source_target_pairs={{0,8},{4,12},{8,16},{12,20},{16,24},{20,28},{24,32},{28,36},{32,40... | collective-permute-start | bytes 786440 | tf_op jit(solution)/shard_map/ppermute | solution.py:236
  8.1 13.6 %collective-permute-start.1 = (bf16[256,512]{1,0:T(8,128)(2,1)S(1)}, bf16[256,512]{1,0:T(8,128)(2,1)S(1)}, u32[]{:S(2)}, u32[]{:S(2)}) collective-permute-start(bf16[256,512]{1,0:T(8,128)(2,1)S(1)} %get-tuple-element.38), channel_id=1, source_target_pairs={{0,12},{4,8},{8,20},{12,16},{16,28},{20,24},{24,36},{28,32},{32,44... | collective-permute-start | bytes 786440 | tf_op jit(solution)/shard_map/ppermute | solution.py:236
  15.6 38.5 %copy-start.6 = (bf16[256,512]{1,0:T(8,128)(2,1)}, bf16[256,512]{1,0:T(8,128)(2,1)S(1)}, u32[]{:S(2)}) copy-start(bf16[256,512]{1,0:T(8,128)(2,1)S(1)} %collective-permute-done.5.kv) | copy-start | bytes 786436
  15.7 11.2 %collective-permute-start.6 = (bf16[256,512]{1,0:T(8,128)(2,1)S(1)}, bf16[256,512]{1,0:T(8,128)(2,1)S(1)}, u32[]{:S(2)}, u32[]{:S(2)}) collective-permute-start(bf16[256,512]{1,0:T(8,128)(2,1)S(1)} %collective-permute-done.5.kv), channel_id=1, source_target_pairs={{0,8},{4,12},{8,16},{12,20},{16,24},{20,28},{24,32},{28,36},{32,40... | collective-permute-start | bytes 786440 | tf_op jit(solution)/shard_map/ppermute | solution.py:240
  21.8 32.4 %copy-start.5 = (bf16[256,512]{1,0:T(8,128)(2,1)}, bf16[256,512]{1,0:T(8,128)(2,1)S(1)}, u32[]{:S(2)}) copy-start(bf16[256,512]{1,0:T(8,128)(2,1)S(1)} %collective-permute-done.1.kv) | copy-start | bytes 786436
  21.8 10.7 %collective-permute-start.2 = (bf16[256,512]{1,0:T(8,128)(2,1)S(1)}, bf16[256,512]{1,0:T(8,128)(2,1)S(1)}, u32[]{:S(2)}, u32[]{:S(2)}) collective-permute-start(bf16[256,512]{1,0:T(8,128)(2,1)S(1)} %collective-permute-done.1.kv), channel_id=1, source_target_pairs={{0,8},{4,12},{8,16},{12,20},{16,24},{20,28},{24,32},{28,36},{32,40... | collective-permute-start | bytes 786440 | tf_op jit(solution)/shard_map/ppermute | solution.py:240
  26.9 27.3 %copy-start.8 = (bf16[256,512]{1,0:T(8,128)(2,1)}, bf16[256,512]{1,0:T(8,128)(2,1)S(1)}, u32[]{:S(2)}) copy-start(bf16[256,512]{1,0:T(8,128)(2,1)S(1)} %collective-permute-done.6.kv) | copy-start | bytes 786436
  26.9 12.6 %collective-permute-start.7 = (bf16[256,512]{1,0:T(8,128)(2,1)S(1)}, bf16[256,512]{1,0:T(8,128)(2,1)S(1)}, u32[]{:S(2)}, u32[]{:S(2)}) collective-permute-start(bf16[256,512]{1,0:T(8,128)(2,1)S(1)} %collective-permute-done.6.kv), channel_id=1, source_target_pairs={{0,8},{4,12},{8,16},{12,20},{16,24},{20,28},{24,32},{28,36},{32,40... | collective-permute-start | bytes 786440 | tf_op jit(solution)/shard_map/ppermute | solution.py:240
  32.5 21.7 %copy-start.7 = (bf16[256,512]{1,0:T(8,128)(2,1)}, bf16[256,512]{1,0:T(8,128)(2,1)S(1)}, u32[]{:S(2)}) copy-start(bf16[256,512]{1,0:T(8,128)(2,1)S(1)} %collective-permute-done.2.kv) | copy-start | bytes 786436
  32.5 11.2 %collective-permute-start.3 = (bf16[256,512]{1,0:T(8,128)(2,1)S(1)}, bf16[256,512]{1,0:T(8,128)(2,1)S(1)}, u32[]{:S(2)}, u32[]{:S(2)}) collective-permute-start(bf16[256,512]{1,0:T(8,128)(2,1)S(1)} %collective-permute-done.2.kv), channel_id=1, source_target_pairs={{0,8},{4,12},{8,16},{12,20},{16,24},{20,28},{24,32},{28,36},{32,40... | collective-permute-start | bytes 786440 | tf_op jit(solution)/shard_map/ppermute | solution.py:240
  39.5 20.6 %copy-start.10 = (bf16[256,512]{1,0:T(8,128)(2,1)}, bf16[256,512]{1,0:T(8,128)(2,1)S(1)}, u32[]{:S(2)}) copy-start(bf16[256,512]{1,0:T(8,128)(2,1)S(1)} %collective-permute-done.7.kv) | copy-start | bytes 786436
  39.5 45.1 %collective-permute-start.8 = (bf16[256,512]{1,0:T(8,128)(2,1)S(1)}, bf16[256,512]{1,0:T(8,128)(2,1)S(1)}, u32[]{:S(2)}, u32[]{:S(2)}) collective-permute-start(bf16[256,512]{1,0:T(8,128)(2,1)S(1)} %collective-permute-done.7.kv), channel_id=1, source_target_pairs={{0,8},{4,12},{8,16},{12,20},{16,24},{20,28},{24,32},{28,36},{32,40... | collective-permute-start | bytes 786440 | tf_op jit(solution)/shard_map/ppermute | solution.py:240
  43.7 16.3 %copy-start.9 = (bf16[256,512]{1,0:T(8,128)(2,1)}, bf16[256,512]{1,0:T(8,128)(2,1)S(1)}, u32[]{:S(2)}) copy-start(bf16[256,512]{1,0:T(8,128)(2,1)S(1)} %collective-permute-done.3.kv) | copy-start | bytes 786436
  43.7 46.5 %collective-permute-start.4 = (bf16[256,512]{1,0:T(8,128)(2,1)S(1)}, bf16[256,512]{1,0:T(8,128)(2,1)S(1)}, u32[]{:S(2)}, u32[]{:S(2)}) collective-permute-start(bf16[256,512]{1,0:T(8,128)(2,1)S(1)} %collective-permute-done.3.kv), channel_id=1, source_target_pairs={{0,8},{4,12},{8,16},{12,20},{16,24},{20,28},{24,32},{28,36},{32,40... | collective-permute-start | bytes 786440 | tf_op jit(solution)/shard_map/ppermute | solution.py:240
  54.2 1.0 copy-start
  84.6 0.7 copy-start.12
  90.2 0.7 copy-start.11
  95.1 7.6 %collective-permute-start.9 = (bf16[256,1024]{1,0:T(8,128)(2,1)S(1)}, bf16[256,1024]{1,0:T(8,128)(2,1)S(1)}, u32[]{:S(2)}, u32[]{:S(2)}) collective-permute-start(bf16[256,1024]{1,0:T(8,128)(2,1)S(1)} %get-tuple-element.64), channel_id=1, source_target_pairs={{0,4},{4,0},{8,12},{12,8},{16,20},{20,16},{24,28},{28,24},{32,36},... | collective-permute-start | bytes 1572872 | tf_op jit(solution)/shard_map/ppermute | solution.py:269

commit v2 on v1

--- a/solution.py
+++ b/solution.py
@@ -17,7 +17,8 @@
 LOG2E = math.log2(math.e)
 FACTOR = HD**-0.5 * LOG2E
 NEG = -1e30
-VLIM = 48 * 1024 * 1024
+COSTS = (5.0, 4.0)
+VLIM = 32 * 1024 * 1024
 
 
 def vmem(shape, dtype):
@@ -110,7 +111,7 @@
     lax.fori_loop(blocks[0], blocks[1], body, 0)
 
 
-def first_kernel(meta, lo, q, near, recv, qcat, acc, top, low):
+def first_kernel(meta, lo, q, near, recv, qcat, acc, top, low, token):
     core = meta[0]
     qcat[0:ROWS, :] = q[:, pl.ds(pl.multiple_of(core * HALF, HALF), HALF)]
     qcat[ROWS : 2 * ROWS, :] = recv[:, 0:HALF]
@@ -129,7 +130,7 @@
     chunk_update(meta, qcat, near, 0, lo, own_base, acc, top, low, (2, 4))
 
 
-def next_kernel(step, cross, meta, lo, q, kv, acc_in, top_in, low_in, acc, top, low):
+def next_kernel(step, cross, meta, lo, q, kv, acc_in, top_in, low_in, acc, top, low, *token):
     base = meta[3 if cross else 1] - step * 2 * ROWS
     chunk_update(meta, q, kv, 0, lo, base, acc, top, low, (0, 4))
 
@@ -171,12 +172,30 @@
 STATE = [vmem((2 * ROWS, HALF), jnp.float32)] * 3
 
 
-def cost(tiles):
+TOKEN = [vmem((8, 128), jnp.float32)]
+ASPEC = pl.BlockSpec(memory_space=pl.ANY)
+
+
+def touch(buffer, token):
+    return pl.pallas_call(
+        lambda buffer_ref, token_ref, out_ref: None,
+        out_shape=vmem(buffer.shape, buffer.dtype),
+        in_specs=[ASPEC, ASPEC],
+        out_specs=ASPEC,
+        input_output_aliases={0: 0},
+        compiler_params=pltpu.CompilerParams(vmem_limit_bytes=1024 * 1024),
+        name="touch",
+    )(near_core(buffer), near_core(token))
+
+
+def cost(micros):
     return pl.CostEstimate(
-        flops=tiles * 4 * ROWS * ROWS * HD * HEADS,
-        bytes_accessed=1 << 20,
-        transcendentals=tiles * ROWS * ROWS * HEADS,
+        flops=int(micros * 1.15e9), bytes_accessed=1 << 20, transcendentals=1 << 20
     )
+
+
+def near_core(x):
+    return pltpu.with_memory_space_constraint(x, pltpu.VMEM)
 
 
 def local(queries, keys, values, lengths, home):
@@ -233,38 +252,41 @@
     other = [(i, (i ^ 1) + 2) for i in range(count - 2)]
     pair = [(i, i ^ 1) for i in range(count)]
     shift = functools.partial(lax.ppermute, axis_name="seq")
-    chunks = [[shift(near, perm=same)], [shift(cross, perm=other)]]
+    arrived = [shift(near, perm=same), shift(cross, perm=other)]
     recv = shift(swap, perm=pair)
-    for step in range(1, 4):
-        for chain in chunks:
-            chain.append(shift(chain[-1], perm=same))
 
     qcat, *state = pl.pallas_call(
         first_kernel,
-        out_shape=[vmem((2 * ROWS, HALF), jnp.bfloat16)] + STATE,
+        out_shape=[vmem((2 * ROWS, HALF), jnp.bfloat16)] + STATE + TOKEN,
         in_specs=[SSPEC] + [VSPEC] * 4,
-        out_specs=[VSPEC] * 4,
+        out_specs=[VSPEC] * 4 + [ASPEC],
         compiler_params=params(),
-        cost_estimate=cost(3),
+        cost_estimate=cost(COSTS[0]),
         name="first",
-    )(meta, lo, queries, near, recv)
-    for step in range(4):
-        for side in range(2):
-            last = step == 3 and side == 1
-            kernel = last_kernel if last else next_kernel
-            extra = [vmem((ROWS, HALF), jnp.bfloat16)] * 2 if last else []
-            kv = chunks[side][step]
-            results = pl.pallas_call(
-                functools.partial(kernel, step + 1, side == 1),
-                out_shape=extra + STATE,
-                in_specs=[SSPEC] + [VSPEC] * 6,
-                out_specs=[VSPEC] * (3 + len(extra)),
-                input_output_aliases={4: len(extra), 5: len(extra) + 1, 6: len(extra) + 2},
-                compiler_params=params(),
-                cost_estimate=cost(2),
-                name="last" if last else "next",
-            )(meta, lo, qcat, kv, *state)
-            state = results[len(extra) :]
+    )(meta, near_core(lo), queries, near_core(near), near_core(recv))
+    token = state.pop()
+    for index in range(8):
+        step, side = index // 2, index % 2
+        last = index == 7
+        kv = arrived[index]
+        if index < 6:
+            held = touch(kv, token)
+            arrived.append(shift(held, perm=same))
+            kv = held
+        kernel = last_kernel if last else next_kernel
+        extra = [vmem((ROWS, HALF), jnp.bfloat16)] * 2 if last else []
+        results = pl.pallas_call(
+            functools.partial(kernel, step + 1, side == 1),
+            out_shape=extra + STATE + ([] if last else TOKEN),
+            in_specs=[SSPEC] + [VSPEC] * 6,
+            out_specs=[VSPEC] * (3 + len(extra)) + ([] if last else [ASPEC]),
+            input_output_aliases={4: len(extra), 5: len(extra) + 1, 6: len(extra) + 2},
+            compiler_params=params(),
+            cost_estimate=cost(COSTS[1]),
+            name="last" if last else "next",
+        )(meta, near_core(lo), near_core(qcat), near_core(kv), *[near_core(x) for x in state])
+        state = results[len(extra) : len(extra) + 3]
+        token = results[-1]
     keep, send = results[:2]
     got = shift(send, perm=pair)
     return pl.pallas_call(
@@ -274,7 +296,7 @@
         out_specs=VSPEC,
         compiler_params=params(),
         name="join",
-    )(core[None].astype(jnp.int32), keep, got)
+    )(core[None].astype(jnp.int32), near_core(keep), near_core(got))
 
 
 def solution(mesh):

time: 104 us -> 80.9 us (0.78)
  the two profiles are of different devices: /device:TPU:441 before, /device:TPU:449 now
where the time goes in v2:
time: 80.9 us; the launch traced here: 80.4 us
  Pallas kernels  39.9 us (49%)
  starting transfers between devices  30 us (37%)
  local copies, waits for them, and re-layouts  5.13 us (6%)
  other arithmetic  2.73 us (3%)
  waiting for transfers between devices  2.33 us (3%)
    pallas_call x8, Pallas kernels, local(): pl.pallas_call(functools.partial(kernel, step + 1, side == 1), out_shape=...  31.7 us
    ppermute x6, starting transfers between devices, local(): arrived.append(shift(held, perm=same))  15.6 us
    ppermute x2, starting transfers between devices, local(): arrived = [shift(near, perm=same), shift(cross, perm=other)]  6.96 us
    pallas_call x1, Pallas kernels, local(): pl.pallas_call(first_kernel, out_shape=[vmem((2 * ROWS, HALF), jnp.bfloat...  6.22 us
    ppermute x1, starting transfers between devices, local(): got = shift(send, perm=pair)  5.42 us
    unnamed x10, local copies, waits for them, and re-layouts  3.14 us
    ppermute x1, starting transfers between devices, local(): recv = shift(swap, perm=pair)  2.02 us
  transfers between devices with their start and end apart: 10, of which 2 were waited for; matrix products, arithmetic and copies ran while one was open for 6% of the time, Pallas kernels for 43%

profile of v2, /device:TPU:449, one launch (start us, length us, event | category | flops | bytes accessed | tf_op | source)
XLA Modules:
  0.0 80.4 jit_solution(17967630218356635023)
XLA Ops:
  0.0 1.2 %copy-done = bf16[256,2048]{1,0:T(8,128)(2,1)S(1)} copy-done((bf16[256,2048]{1,0:T(8,128)(2,1)S(1)}, bf16[256,2048]{1,0:T(8,128)(2,1)}, u32[]{:S(2)}) %copy-start) | copy-done | bytes 1048600
  1.2 0.9 %copy-done.2 = bf16[256,512]{1,0:T(8,128)(2,1)S(1)} copy-done((bf16[256,512]{1,0:T(8,128)(2,1)S(1)}, bf16[256,512]{1,0:T(8,128)(2,1)}, u32[]{:S(2)}) %copy-start.2) | copy-done | bytes 262168
  2.2 0.9 %copy-done.3 = bf16[256,512]{1,0:T(8,128)(2,1)S(1)} copy-done((bf16[256,512]{1,0:T(8,128)(2,1)S(1)}, bf16[256,512]{1,0:T(8,128)(2,1)}, u32[]{:S(2)}) %copy-start.3) | copy-done | bytes 262168
  3.1 0.9 %pack.1 = (bf16[256,512]{1,0:T(8,128)(2,1)}, bf16[256,512]{1,0:T(8,128)(2,1)}, bf16[256,1536]{1,0:T(8,128)(2,1)S(1)}) custom-call(s32[1]{0:T(128)} %bitcast.meta, bf16[256,2048]{1,0:T(8,128)(2,1)S(1)} %copy-done, bf16[256,512]{1,0:T(8,128)(2,1)S(1)} %copy-done.2, bf16[256,512]{1,0:T(8,128)(2,1)S(1)} %copy-done.3), custom_call_target="tpu_custom_call" | custom-call | tf_op jit(solution)/shard_map/pack/pallas_call | solution.py:238
  4.0 3.8 %collective-permute-start.1 = (bf16[256,512]{1,0:T(8,128)(2,1)}, bf16[256,512]{1,0:T(8,128)(2,1)S(1)}, u32[]{:S(2)}, u32[]{:S(2)}) collective-permute-start(bf16[256,512]{1,0:T(8,128)(2,1)} %get-tuple-element.44), channel_id=1, source_target_pairs={{0,12},{4,8},{8,20},{12,16},{16,28},{20,24},{24,36},{28,32},{32,44... | collective-permute-start | bytes 786440 | tf_op jit(solution)/shard_map/ppermute | solution.py:255
  7.8 3.2 %collective-permute-start.2 = (bf16[256,512]{1,0:T(8,128)(2,1)}, bf16[256,512]{1,0:T(8,128)(2,1)S(1)}, u32[]{:S(2)}, u32[]{:S(2)}) collective-permute-start(bf16[256,512]{1,0:T(8,128)(2,1)} %get-tuple-element.41.near), channel_id=1, source_target_pairs={{0,8},{4,12},{8,16},{12,20},{16,24},{20,28},{24,32},{28,36},{32,40... | collective-permute-start | bytes 786440 | tf_op jit(solution)/shard_map/ppermute | solution.py:255
  11.0 2.0 %collective-permute-start = (bf16[256,1536]{1,0:T(8,128)(2,1)S(1)}, bf16[256,1536]{1,0:T(8,128)(2,1)S(1)}, u32[]{:S(2)}, u32[]{:S(2)}) collective-permute-start(bf16[256,1536]{1,0:T(8,128)(2,1)S(1)} %get-tuple-element.42), channel_id=1, source_target_pairs={{0,4},{4,0},{8,12},{12,8},{16,20},{20,16},{24,28},{28,24},{32,36},... | collective-permute-start | bytes 2359304 | tf_op jit(solution)/shard_map/ppermute | solution.py:256
  13.1 0.8 select_reduce_fusion.1
  13.8 0.1 pad_add_fusion
  13.9 0.1 fusion.1
  14.0 0.2 select_reduce_fusion
  14.2 0.1 fusion
  14.3 0.9 %copy.42 = s32[512,1]{1,0:T(8,128)} copy(s32[512,1]{0,1:T(1,128)S(1)} %bitcast.12) | data formatting | bytes 4096 | tf_op jit(solution)/shard_map/sub | solution.py:214
  15.2 0.9 %copy.41 = s32[512,1]{1,0:T(8,128)} copy(s32[512,1]{0,1:T(1,128)S(1)} %bitcast.11) | data formatting | bytes 4096 | tf_op jit(solution)/shard_map/reduce_max | solution.py:213
  16.0 1.1 %max.14.lo = s32[512,1]{1,0:T(8,128)S(1)} maximum(s32[512,1]{1,0:T(8,128)} %copy.41, s32[512,1]{1,0:T(8,128)} %copy.42) | non-fusion elementwise | flops 512 | bytes 6144 | tf_op jit(solution)/shard_map/max | solution.py:214
  17.1 0.0 copy-done.4
  17.1 0.1 compare_convert_fusion
  17.2 0.2 slice_reduce_fusion
  17.4 0.2 convert_reduce_fusion
  17.6 0.2 select_reduce_fusion.2
  17.7 0.1 concatenate.4.meta
  17.8 0.0 collective-permute-done.recv
  17.8 6.2 %first.1 = (bf16[512,1024]{1,0:T(8,128)(2,1)S(1)}, f32[512,1024]{1,0:T(8,128)S(1)}, f32[512,1024]{1,0:T(8,128)S(1)}, f32[512,1024]{1,0:T(8,128)S(1)}, f32[8,128]{1,0:T(8,128)S(1)}) custom-call(s32[21]{0:T(128)S(1)} %concatenate.4.meta, s32[512,1]{1,0:T(8,128)S(1)} %max.14.lo, bf16[256,2048]{1,0:T(8,128)(2,1)S(1)} %copy-done.1, ...), custom_call_target="tpu_custom_call" | custom-call | flops 5750000128 | bytes 1048576 | tf_op jit(solution)/shard_map/first/pallas_call | solution.py:258
  24.1 0.0 collective-permute-done.2.buffer_ref
  24.1 3.2 %collective-permute-start.4 = (bf16[256,512]{1,0:T(8,128)(2,1)S(1)}, bf16[256,512]{1,0:T(8,128)(2,1)S(1)}, u32[]{:S(2)}, u32[]{:S(2)}) collective-permute-start(bf16[256,512]{1,0:T(8,128)(2,1)S(1)} %touch.6.kv), channel_id=1, source_target_pairs={{0,8},{4,12},{8,16},{12,20},{16,24},{20,28},{24,32},{28,36},{32,40... | collective-permute-start | bytes 786440 | tf_op jit(solution)/shard_map/ppermute | solution.py:274
  27.3 4.0 %next.7 = (f32[512,1024]{1,0:T(8,128)S(1)}, f32[512,1024]{1,0:T(8,128)S(1)}, f32[512,1024]{1,0:T(8,128)S(1)}, f32[8,128]{1,0:T(8,128)S(1)}) custom-call(s32[21]{0:T(128)S(1)} %concatenate.4.meta, s32[512,1]{1,0:T(8,128)S(1)} %max.14.lo, bf16[512,1024]{1,0:T(8,128)(2,1)S(1)} %get-tuple-element.43.q, ...), custom_call_target="tpu_custom_call", output_to_operand_aliasing={{0}: (4, {}), {1}: (5, {}), {2}: (6, {})} | custom-call | flops 4600000000 | bytes 1048576 | tf_op jit(solution)/shard_map/next/pallas_call | solution.py:278
  31.4 0.0 collective-permute-done.1.buffer_ref
  31.4 4.4 %collective-permute-start.3 = (bf16[256,512]{1,0:T(8,128)(2,1)S(1)}, bf16[256,512]{1,0:T(8,128)(2,1)S(1)}, u32[]{:S(2)}, u32[]{:S(2)}) collective-permute-start(bf16[256,512]{1,0:T(8,128)(2,1)S(1)} %touch.7.kv), channel_id=1, source_target_pairs={{0,8},{4,12},{8,16},{12,20},{16,24},{20,28},{24,32},{28,36},{32,40... | collective-permute-start | bytes 786440 | tf_op jit(solution)/shard_map/ppermute | solution.py:274
  35.8 4.1 %next.8 = (f32[512,1024]{1,0:T(8,128)S(1)}, f32[512,1024]{1,0:T(8,128)S(1)}, f32[512,1024]{1,0:T(8,128)S(1)}, f32[8,128]{1,0:T(8,128)S(1)}) custom-call(s32[21]{0:T(128)S(1)} %concatenate.4.meta, s32[512,1]{1,0:T(8,128)S(1)} %max.14.lo, bf16[512,1024]{1,0:T(8,128)(2,1)S(1)} %get-tuple-element.43.q, ...), custom_call_target="tpu_custom_call", output_to_operand_aliasing={{0}: (4, {}), {1}: (5, {}), {2}: (6, {})} | custom-call | flops 4600000000 | bytes 1048576 | tf_op jit(solution)/shard_map/next/pallas_call | solution.py:278
  39.9 0.0 collective-permute-done.4.buffer_ref
  39.9 1.9 %collective-permute-start.6 = (bf16[256,512]{1,0:T(8,128)(2,1)S(1)}, bf16[256,512]{1,0:T(8,128)(2,1)S(1)}, u32[]{:S(2)}, u32[]{:S(2)}) collective-permute-start(bf16[256,512]{1,0:T(8,128)(2,1)S(1)} %touch.8.kv), channel_id=1, source_target_pairs={{0,8},{4,12},{8,16},{12,20},{16,24},{20,28},{24,32},{28,36},{32,40... | collective-permute-start | bytes 786440 | tf_op jit(solution)/shard_map/ppermute | solution.py:274
  41.9 4.0 %next.9 = (f32[512,1024]{1,0:T(8,128)S(1)}, f32[512,1024]{1,0:T(8,128)S(1)}, f32[512,1024]{1,0:T(8,128)S(1)}, f32[8,128]{1,0:T(8,128)S(1)}) custom-call(s32[21]{0:T(128)S(1)} %concatenate.4.meta, s32[512,1]{1,0:T(8,128)S(1)} %max.14.lo, bf16[512,1024]{1,0:T(8,128)(2,1)S(1)} %get-tuple-element.43.q, ...), custom_call_target="tpu_custom_call", output_to_operand_aliasing={{0}: (4, {}), {1}: (5, {}), {2}: (6, {})} | custom-call | flops 4600000000 | bytes 1048576 | tf_op jit(solution)/shard_map/next/pallas_call | solution.py:278
  45.9 0.0 collective-permute-done.3.buffer_ref
  45.9 1.9 %collective-permute-start.5 = (bf16[256,512]{1,0:T(8,128)(2,1)S(1)}, bf16[256,512]{1,0:T(8,128)(2,1)S(1)}, u32[]{:S(2)}, u32[]{:S(2)}) collective-permute-start(bf16[256,512]{1,0:T(8,128)(2,1)S(1)} %touch.9.kv), channel_id=1, source_target_pairs={{0,8},{4,12},{8,16},{12,20},{16,24},{20,28},{24,32},{28,36},{32,40... | collective-permute-start | bytes 786440 | tf_op jit(solution)/shard_map/ppermute | solution.py:274
  47.9 4.0 %next.10 = (f32[512,1024]{1,0:T(8,128)S(1)}, f32[512,1024]{1,0:T(8,128)S(1)}, f32[512,1024]{1,0:T(8,128)S(1)}, f32[8,128]{1,0:T(8,128)S(1)}) custom-call(s32[21]{0:T(128)S(1)} %concatenate.4.meta, s32[512,1]{1,0:T(8,128)S(1)} %max.14.lo, bf16[512,1024]{1,0:T(8,128)(2,1)S(1)} %get-tuple-element.43.q, ...), custom_call_target="tpu_custom_call", output_to_operand_aliasing={{0}: (4, {}), {1}: (5, {}), {2}: (6, {})} | custom-call | flops 4600000000 | bytes 1048576 | tf_op jit(solution)/shard_map/next/pallas_call | solution.py:278
  52.0 0.0 collective-permute-done.6.buffer_ref
  52.0 2.1 %collective-permute-start.8 = (bf16[256,512]{1,0:T(8,128)(2,1)S(1)}, bf16[256,512]{1,0:T(8,128)(2,1)S(1)}, u32[]{:S(2)}, u32[]{:S(2)}) collective-permute-start(bf16[256,512]{1,0:T(8,128)(2,1)S(1)} %touch.10.kv), channel_id=1, source_target_pairs={{0,8},{4,12},{8,16},{12,20},{16,24},{20,28},{24,32},{28,36},{32,40... | collective-permute-start | bytes 786440 | tf_op jit(solution)/shard_map/ppermute | solution.py:274
  54.1 4.0 %next.11 = (f32[512,1024]{1,0:T(8,128)S(1)}, f32[512,1024]{1,0:T(8,128)S(1)}, f32[512,1024]{1,0:T(8,128)S(1)}, f32[8,128]{1,0:T(8,128)S(1)}) custom-call(s32[21]{0:T(128)S(1)} %concatenate.4.meta, s32[512,1]{1,0:T(8,128)S(1)} %max.14.lo, bf16[512,1024]{1,0:T(8,128)(2,1)S(1)} %get-tuple-element.43.q, ...), custom_call_target="tpu_custom_call", output_to_operand_aliasing={{0}: (4, {}), {1}: (5, {}), {2}: (6, {})} | custom-call | flops 4600000000 | bytes 1048576 | tf_op jit(solution)/shard_map/next/pallas_call | solution.py:278
  58.2 0.0 collective-permute-done.5.buffer_ref
  58.2 1.9 %collective-permute-start.7 = (bf16[256,512]{1,0:T(8,128)(2,1)S(1)}, bf16[256,512]{1,0:T(8,128)(2,1)S(1)}, u32[]{:S(2)}, u32[]{:S(2)}) collective-permute-start(bf16[256,512]{1,0:T(8,128)(2,1)S(1)} %touch.11.kv), channel_id=1, source_target_pairs={{0,8},{4,12},{8,16},{12,20},{16,24},{20,28},{24,32},{28,36},{32,40... | collective-permute-start | bytes 786440 | tf_op jit(solution)/shard_map/ppermute | solution.py:274
  60.1 4.1 %next.12 = (f32[512,1024]{1,0:T(8,128)S(1)}, f32[512,1024]{1,0:T(8,128)S(1)}, f32[512,1024]{1,0:T(8,128)S(1)}, f32[8,128]{1,0:T(8,128)}) custom-call(s32[21]{0:T(128)S(1)} %concatenate.4.meta, s32[512,1]{1,0:T(8,128)S(1)} %max.14.lo, bf16[512,1024]{1,0:T(8,128)(2,1)S(1)} %get-tuple-element.43.q, ...), custom_call_target="tpu_custom_call", output_to_operand_aliasing={{0}: (4, {}), {1}: (5, {}), {2}: (6, {})} | custom-call | flops 4600000000 | bytes 1048576 | tf_op jit(solution)/shard_map/next/pallas_call | solution.py:278
  64.2 0.0 collective-permute-done.8.kv
  64.2 4.1 %next.13 = (f32[512,1024]{1,0:T(8,128)S(1)}, f32[512,1024]{1,0:T(8,128)S(1)}, f32[512,1024]{1,0:T(8,128)S(1)}, f32[8,128]{1,0:T(8,128)}) custom-call(s32[21]{0:T(128)S(1)} %concatenate.4.meta, s32[512,1]{1,0:T(8,128)S(1)} %max.14.lo, bf16[512,1024]{1,0:T(8,128)(2,1)S(1)} %get-tuple-element.43.q, ...), custom_call_target="tpu_custom_call", output_to_operand_aliasing={{0}: (4, {}), {1}: (5, {}), {2}: (6, {})} | custom-call | flops 4600000000 | bytes 1048576 | tf_op jit(solution)/shard_map/next/pallas_call | solution.py:278
  68.3 0.8 collective-permute-done.7.kv
  69.1 3.3 %last.1 = (bf16[256,1024]{1,0:T(8,128)(2,1)S(1)}, bf16[256,1024]{1,0:T(8,128)(2,1)S(1)}, f32[512,1024]{1,0:T(8,128)S(1)}, f32[512,1024]{1,0:T(8,128)S(1)}, f32[512,1024]{1,0:T(8,128)S(1)}) custom-call(s32[21]{0:T(128)S(1)} %concatenate.4.meta, s32[512,1]{1,0:T(8,128)S(1)} %max.14.lo, ...), custom_call_target="tpu_custom_call", output_to_operand_aliasing={{2}: (4, {}), {3}: (5, {}), {4}: (6, {})} | custom-call | flops 4600000000 | bytes 1048576 | tf_op jit(solution)/shard_map/last/pallas_call | solution.py:278
  72.4 5.4 %collective-permute-start.9 = (bf16[256,1024]{1,0:T(8,128)(2,1)S(1)}, bf16[256,1024]{1,0:T(8,128)(2,1)S(1)}, u32[]{:S(2)}, u32[]{:S(2)}) collective-permute-start(bf16[256,1024]{1,0:T(8,128)(2,1)S(1)} %get-tuple-element.76), channel_id=1, source_target_pairs={{0,4},{4,0},{8,12},{12,8},{16,20},{20,16},{24,28},{28,24},{32,36},... | collective-permute-start | bytes 1572872 | tf_op jit(solution)/shard_map/ppermute | solution.py:291
  77.9 1.5 %collective-permute-done.9.recv = bf16[256,1024]{1,0:T(8,128)(2,1)S(1)} collective-permute-done((bf16[256,1024]{1,0:T(8,128)(2,1)S(1)}, bf16[256,1024]{1,0:T(8,128)(2,1)S(1)}, u32[]{:S(2)}, u32[]{:S(2)}) %collective-permute-start.9) | collective-permute-done | bytes 524320 | tf_op jit(solution)/shard_map/ppermute | solution.py:291
  79.4 1.0 %join.1 = bf16[256,2048]{1,0:T(8,128)(2,1)} custom-call(s32[1]{0:T(128)} %bitcast.meta, bf16[256,1024]{1,0:T(8,128)(2,1)S(1)} %get-tuple-element.75.keep, bf16[256,1024]{1,0:T(8,128)(2,1)S(1)} %collective-permute-done.9.recv), custom_call_target="tpu_custom_call" | custom-call | tf_op jit(solution)/shard_map/join/pallas_call | solution.py:292
  (13 shorter events, 0.0 us)
Async XLA Ops:
  0.0 17.1 %copy-start.4 = (s32[256]{0:T(256)S(1)}, s32[256]{0:T(256)}, u32[]{:S(2)}) copy-start(s32[256]{0:T(256)} %param.9) | copy-start | bytes 3076
  0.0 1.2 %copy-start = (bf16[256,2048]{1,0:T(8,128)(2,1)S(1)}, bf16[256,2048]{1,0:T(8,128)(2,1)}, u32[]{:S(2)}) copy-start(bf16[256,2048]{1,0:T(8,128)(2,1)} %q.3) | copy-start | bytes 3145732
  1.2 0.9 %copy-start.2 = (bf16[256,512]{1,0:T(8,128)(2,1)S(1)}, bf16[256,512]{1,0:T(8,128)(2,1)}, u32[]{:S(2)}) copy-start(bf16[256,512]{1,0:T(8,128)(2,1)} %k.1) | copy-start | bytes 786436
  2.2 0.9 %copy-start.3 = (bf16[256,512]{1,0:T(8,128)(2,1)S(1)}, bf16[256,512]{1,0:T(8,128)(2,1)}, u32[]{:S(2)}) copy-start(bf16[256,512]{1,0:T(8,128)(2,1)} %v.1) | copy-start | bytes 786436
  3.1 14.7 %copy-start.1 = (bf16[256,2048]{1,0:T(8,128)(2,1)S(1)}, bf16[256,2048]{1,0:T(8,128)(2,1)}, u32[]{:S(2)}) copy-start(bf16[256,2048]{1,0:T(8,128)(2,1)} %q.3) | copy-start | bytes 3145732
  4.0 27.3 %collective-permute-start.1 = (bf16[256,512]{1,0:T(8,128)(2,1)}, bf16[256,512]{1,0:T(8,128)(2,1)S(1)}, u32[]{:S(2)}, u32[]{:S(2)}) collective-permute-start(bf16[256,512]{1,0:T(8,128)(2,1)} %get-tuple-element.44), channel_id=1, source_target_pairs={{0,12},{4,8},{8,20},{12,16},{16,28},{20,24},{24,36},{28,32},{32,44... | collective-permute-start | bytes 786440 | tf_op jit(solution)/shard_map/ppermute | solution.py:255
  7.8 16.3 %collective-permute-start.2 = (bf16[256,512]{1,0:T(8,128)(2,1)}, bf16[256,512]{1,0:T(8,128)(2,1)S(1)}, u32[]{:S(2)}, u32[]{:S(2)}) collective-permute-start(bf16[256,512]{1,0:T(8,128)(2,1)} %get-tuple-element.41.near), channel_id=1, source_target_pairs={{0,8},{4,12},{8,16},{12,20},{16,24},{20,28},{24,32},{28,36},{32,40... | collective-permute-start | bytes 786440 | tf_op jit(solution)/shard_map/ppermute | solution.py:255
  11.0 6.8 %collective-permute-start = (bf16[256,1536]{1,0:T(8,128)(2,1)S(1)}, bf16[256,1536]{1,0:T(8,128)(2,1)S(1)}, u32[]{:S(2)}, u32[]{:S(2)}) collective-permute-start(bf16[256,1536]{1,0:T(8,128)(2,1)S(1)} %get-tuple-element.42), channel_id=1, source_target_pairs={{0,4},{4,0},{8,12},{12,8},{16,20},{20,16},{24,28},{28,24},{32,36},... | collective-permute-start | bytes 2359304 | tf_op jit(solution)/shard_map/ppermute | solution.py:256
  24.1 15.8 %collective-permute-start.4 = (bf16[256,512]{1,0:T(8,128)(2,1)S(1)}, bf16[256,512]{1,0:T(8,128)(2,1)S(1)}, u32[]{:S(2)}, u32[]{:S(2)}) collective-permute-start(bf16[256,512]{1,0:T(8,128)(2,1)S(1)} %touch.6.kv), channel_id=1, source_target_pairs={{0,8},{4,12},{8,16},{12,20},{16,24},{20,28},{24,32},{28,36},{32,40... | collective-permute-start | bytes 786440 | tf_op jit(solution)/shard_map/ppermute | solution.py:274
  31.4 14.5 %collective-permute-start.3 = (bf16[256,512]{1,0:T(8,128)(2,1)S(1)}, bf16[256,512]{1,0:T(8,128)(2,1)S(1)}, u32[]{:S(2)}, u32[]{:S(2)}) collective-permute-start(bf16[256,512]{1,0:T(8,128)(2,1)S(1)} %touch.7.kv), channel_id=1, source_target_pairs={{0,8},{4,12},{8,16},{12,20},{16,24},{20,28},{24,32},{28,36},{32,40... | collective-permute-start | bytes 786440 | tf_op jit(solution)/shard_map/ppermute | solution.py:274
  39.9 12.0 %collective-permute-start.6 = (bf16[256,512]{1,0:T(8,128)(2,1)S(1)}, bf16[256,512]{1,0:T(8,128)(2,1)S(1)}, u32[]{:S(2)}, u32[]{:S(2)}) collective-permute-start(bf16[256,512]{1,0:T(8,128)(2,1)S(1)} %touch.8.kv), channel_id=1, source_target_pairs={{0,8},{4,12},{8,16},{12,20},{16,24},{20,28},{24,32},{28,36},{32,40... | collective-permute-start | bytes 786440 | tf_op jit(solution)/shard_map/ppermute | solution.py:274
  45.9 12.2 %collective-permute-start.5 = (bf16[256,512]{1,0:T(8,128)(2,1)S(1)}, bf16[256,512]{1,0:T(8,128)(2,1)S(1)}, u32[]{:S(2)}, u32[]{:S(2)}) collective-permute-start(bf16[256,512]{1,0:T(8,128)(2,1)S(1)} %touch.9.kv), channel_id=1, source_target_pairs={{0,8},{4,12},{8,16},{12,20},{16,24},{20,28},{24,32},{28,36},{32,40... | collective-permute-start | bytes 786440 | tf_op jit(solution)/shard_map/ppermute | solution.py:274
  52.0 12.2 %collective-permute-start.8 = (bf16[256,512]{1,0:T(8,128)(2,1)S(1)}, bf16[256,512]{1,0:T(8,128)(2,1)S(1)}, u32[]{:S(2)}, u32[]{:S(2)}) collective-permute-start(bf16[256,512]{1,0:T(8,128)(2,1)S(1)} %touch.10.kv), channel_id=1, source_target_pairs={{0,8},{4,12},{8,16},{12,20},{16,24},{20,28},{24,32},{28,36},{32,40... | collective-permute-start | bytes 786440 | tf_op jit(solution)/shard_map/ppermute | solution.py:274
  58.2 10.9 %collective-permute-start.7 = (bf16[256,512]{1,0:T(8,128)(2,1)S(1)}, bf16[256,512]{1,0:T(8,128)(2,1)S(1)}, u32[]{:S(2)}, u32[]{:S(2)}) collective-permute-start(bf16[256,512]{1,0:T(8,128)(2,1)S(1)} %touch.11.kv), channel_id=1, source_target_pairs={{0,8},{4,12},{8,16},{12,20},{16,24},{20,28},{24,32},{28,36},{32,40... | collective-permute-start | bytes 786440 | tf_op jit(solution)/shard_map/ppermute | solution.py:274
  72.4 6.9 %collective-permute-start.9 = (bf16[256,1024]{1,0:T(8,128)(2,1)S(1)}, bf16[256,1024]{1,0:T(8,128)(2,1)S(1)}, u32[]{:S(2)}, u32[]{:S(2)}) collective-permute-start(bf16[256,1024]{1,0:T(8,128)(2,1)S(1)} %get-tuple-element.76), channel_id=1, source_target_pairs={{0,4},{4,0},{8,12},{12,8},{16,20},{20,16},{24,28},{28,24},{32,36},... | collective-permute-start | bytes 1572872 | tf_op jit(solution)/shard_map/ppermute | solution.py:291
